TPU v7x, 256 devices: a whole 4x4x8 slice. The times are simulated.
256 devices in a mesh: gx: 16 (over y, x_lo, core), gy: 16 (over z, x_hi).
Axes of the slice: x: 4 (x_hi: 2, x_lo: 2; x = x_hi * 2 + x_lo), y: 4, z: 8, core: 2. Of those that a mesh axis runs over, the one named last changes fastest.
Arguments:
- offsets: bfloat16 [128, 128, 2, 256], P('gx', 'gy'), may hold values from 0 to 1
- vectors: bfloat16 [128, 128, 8, 256], P('gx', 'gy'), may hold values from -6 to 6
- leaf_basis: bfloat16 [128, 128, 32, 256], P('gx', 'gy'), may hold values from -0.375 to 0.375
- couple0: bfloat16 [128, 128, 32, 864], P('gx', 'gy'), may hold values from -0.21875 to 0.21875
- couple1: bfloat16 [64, 64, 32, 864], P('gx', 'gy'), may hold values from -0.21875 to 0.21875
- couple2: bfloat16 [32, 32, 32, 864], P('gx', 'gy'), may hold values from -0.21875 to 0.21875
- couple3: bfloat16 [16, 16, 32, 864], P('gx', 'gy'), may hold values from -0.21875 to 0.21875
- couple4: bfloat16 [8, 8, 32, 864], replicated, may hold values from -0.21875 to 0.21875
- couple_top: bfloat16 [16, 16, 32, 2048], P('gx', 'gy'), may hold values from -0.125 to 0.125
- transfer1: bfloat16 [64, 64, 4, 32, 32], P('gx', 'gy'), may hold values from -0.75 to 0.75
- transfer2: bfloat16 [32, 32, 4, 32, 32], P('gx', 'gy'), may hold values from -0.75 to 0.75
- transfer3: bfloat16 [16, 16, 4, 32, 32], P('gx', 'gy'), may hold values from -0.75 to 0.75
- transfer4: bfloat16 [8, 8, 4, 32, 32], replicated, may hold values from -0.75 to 0.75
Outputs:
- product: float32 [128, 128, 8, 256], P('gx', 'gy')
All inputs are finite; a program needn't handle non-finite values.
Results may differ from a plain program's by a relative error of at most 0.009.
Values may be sent and summed in bfloat16 or wider, within the bound.
A program may use at most 128 MiB of HBM per device.

v0:
```python
import jax
import jax.numpy as jnp
from jax import lax
from jax.sharding import PartitionSpec as P


def with_halo(x, sides, width):
    for axis, dim in sides:
        devices, length = (lax.axis_size(axis), x.shape[dim])
        up = [(i, (i + 1) % devices) for i in range(devices - 1)]
        down = [(j, i) for i, j in up]
        last = lax.slice_in_dim(x, length - width, length, axis=dim)
        first = lax.slice_in_dim(x, 0, width, axis=dim)
        before = lax.ppermute(last, axis, up)
        after = lax.ppermute(first, axis, down)
        x = jnp.concatenate([before, x, after], axis=dim)
    return x


def window_list(par_x, par_y):
    return [
        (a, b)
        for a in range(6)
        for b in range(6)
        if not (abs(a - 2 - par_x) <= 1 and abs(b - 2 - par_y) <= 1)
    ]


def kernel_tile(target, source, shift_x, shift_y):
    delta_x = jnp.float32(shift_x) + (
        target[:, 0, :, None].astype(jnp.float32) - source[:, 0, None, :].astype(jnp.float32)
    )
    delta_y = jnp.float32(shift_y) + (
        target[:, 1, :, None].astype(jnp.float32) - source[:, 1, None, :].astype(jnp.float32)
    )
    radius = jnp.sqrt(delta_x * delta_x + delta_y * delta_y)
    scaled = jnp.float32(1.7320508075688772) * radius
    return (jnp.float32(0.0625) * (1.0 + scaled) * jnp.exp(-scaled)).astype(jnp.bfloat16)


def up_level(child, transfer):
    half_x, half_y = (child.shape[0] // 2, child.shape[1] // 2)
    grouped = child.reshape(half_x, 2, half_y, 2, child.shape[2], child.shape[3])
    grouped = grouped.transpose(0, 2, 1, 3, 4, 5).reshape(
        half_x, half_y, 4, child.shape[2], child.shape[3]
    )
    return jnp.einsum("mnskp,mnsvk->mnvp", transfer, grouped, preferred_element_type=jnp.float32)


def down_level(parent, transfer):
    half_x, half_y = (parent.shape[0], parent.shape[1])
    spread = jnp.einsum("mnskp,mnvp->mnsvk", transfer, parent, preferred_element_type=jnp.float32)
    spread = spread.reshape(half_x, half_y, 2, 2, parent.shape[2], parent.shape[3]).transpose(
        0, 2, 1, 3, 4, 5
    )
    return spread.reshape(2 * half_x, 2 * half_y, parent.shape[2], parent.shape[3])


def far_level(padded, couple):
    size_x, size_y = (couple.shape[0], couple.shape[1])
    nvec, rank = (padded.shape[2], padded.shape[3])
    half_x, half_y = (size_x // 2, size_y // 2)
    rows = []
    for par_x in range(2):
        cols = []
        for par_y in range(2):
            stack = jnp.stack(
                [
                    padded[a : a + 2 * half_x : 2, b : b + 2 * half_y : 2]
                    for a, b in window_list(par_x, par_y)
                ],
                axis=2,
            )
            part = couple[par_x::2, par_y::2].reshape(half_x, half_y, rank, 27, rank)
            cols.append(
                jnp.einsum("mnkjl,mnjvl->mnvk", part, stack, preferred_element_type=jnp.float32)
            )
        rows.append(jnp.stack(cols, axis=2))
    return jnp.stack(rows, axis=1).reshape(size_x, size_y, nvec, rank)


def single_far(whole, box_x, box_y, couple_row):
    nvec, rank = (whole.shape[2], whole.shape[3])
    padded = jnp.pad(whole, ((2, 2), (2, 2), (0, 0), (0, 0)))
    start_x = 2 * (box_x // 2)
    start_y = 2 * (box_y // 2)
    window = lax.dynamic_slice(padded, (start_x, start_y, 0, 0), (6, 6, nvec, rank))
    part = couple_row.reshape(rank, 27, rank)
    results = []
    for par_x in range(2):
        for par_y in range(2):
            stack = jnp.stack([window[a, b] for a, b in window_list(par_x, par_y)], axis=0)
            results.append(
                jnp.einsum("kjl,jvl->vk", part, stack, preferred_element_type=jnp.float32)
            )
    bit_x = box_x % 2
    bit_y = box_y % 2
    first = jnp.where(bit_y == 0, results[0], results[1])
    second = jnp.where(bit_y == 0, results[2], results[3])
    return jnp.where(bit_x == 0, first, second)


def top_single(whole4, anc_x, anc_y, couple_row):
    top_x, top_y, nvec, rank = whole4.shape
    base_x = 2 * (anc_x // 2)
    base_y = 2 * (anc_y // 2)
    other_x = jnp.arange(top_x, dtype=jnp.int32)
    other_y = jnp.arange(top_y, dtype=jnp.int32)
    out_x = (other_x < base_x - 2) | (other_x > base_x + 3)
    out_y = (other_y < base_y - 2) | (other_y > base_y + 3)
    keep = out_x[:, None] | out_y[None, :]
    masked = jnp.where(keep[:, :, None, None], whole4, jnp.zeros_like(whole4))
    masked = masked.reshape(top_x * top_y, nvec, rank)
    part = couple_row.reshape(rank, top_x * top_y, rank)
    return jnp.einsum("kml,mvl->vk", part, masked, preferred_element_type=jnp.float32)


def assemble(gathered, count_x, count_y):
    side = gathered.shape[1]
    width = gathered.shape[3]
    whole = gathered.reshape(count_x, count_y, side, side, width).transpose(0, 2, 1, 3, 4)
    return whole.reshape(count_x * side, count_y * side, width)


def own_window(whole, side, index_x, index_y):
    padded = jnp.pad(whole, ((2, 2), (2, 2), (0, 0)))
    return lax.dynamic_slice(
        padded, (index_x * side, index_y * side, 0), (side + 4, side + 4, whole.shape[2])
    )


def on_device(
    offsets,
    vectors,
    leaf_basis,
    couple0,
    couple1,
    couple2,
    couple3,
    couple4,
    couple_top,
    transfer1,
    transfer2,
    transfer3,
    transfer4,
):
    tile = offsets.shape[0]
    nvec, rank = (vectors.shape[2], leaf_basis.shape[2])
    flat = nvec * rank
    count_x = lax.axis_size("gx")
    count_y = lax.axis_size("gy")
    index_x = lax.axis_index("gx")
    index_y = lax.axis_index("gy")
    pad_off, pad_vec = (
        with_halo(offsets, (("gx", 0), ("gy", 1)), 1),
        with_halo(vectors, (("gx", 0), ("gy", 1)), 1),
    )

    def one_row(row):
        target = lax.dynamic_index_in_dim(offsets, row, 0, keepdims=False)
        total = jnp.zeros((tile, nvec, vectors.shape[3]), jnp.float32)
        for a in range(3):
            src_off = lax.dynamic_index_in_dim(pad_off, row + a, 0, keepdims=False)
            src_vec = lax.dynamic_index_in_dim(pad_vec, row + a, 0, keepdims=False)
            for b in range(3):
                kern = kernel_tile(target, src_off[b : b + tile], 1 - a, 1 - b)
                total = total + jnp.einsum(
                    "tpq,tvq->tvp", kern, src_vec[b : b + tile], preferred_element_type=jnp.float32
                )
        return total

    coef0 = jnp.einsum(
        "ijkp,ijvp->ijvk", leaf_basis, vectors, preferred_element_type=jnp.float32
    ).astype(jnp.bfloat16)
    coef1 = up_level(coef0, transfer1).astype(jnp.bfloat16)
    coef2 = up_level(coef1, transfer2).astype(jnp.bfloat16)
    coef3 = up_level(coef2, transfer3).astype(jnp.bfloat16)
    cycle0 = with_halo(coef0.reshape(tile, tile, flat), (("gx", 0), ("gy", 1)), 2)
    far0 = far_level(cycle0.reshape(tile + 4, tile + 4, nvec, rank), couple0)
    side1 = tile // 2
    side2 = tile // 4
    flat1 = coef1.reshape(1, side1, side1, flat)
    flat2 = coef2.reshape(1, side2, side2, flat)
    flat3 = coef3.reshape(1, 1, 1, flat)
    got1, got2, got3 = (
        lax.all_gather(flat1, ("gx", "gy"), axis=0, tiled=True),
        lax.all_gather(flat2, ("gx", "gy"), axis=0, tiled=True),
        lax.all_gather(flat3, ("gx", "gy"), axis=0, tiled=True),
    )
    cycle1 = own_window(assemble(got1, count_x, count_y), side1, index_x, index_y)
    cycle2 = own_window(assemble(got2, count_x, count_y), side2, index_x, index_y)
    whole3 = assemble(got3, count_x, count_y)
    far1 = far_level(cycle1.reshape(side1 + 4, side1 + 4, nvec, rank), couple1)
    far2 = far_level(cycle2.reshape(side2 + 4, side2 + 4, nvec, rank), couple2)
    whole3 = whole3.reshape(count_x, count_y, nvec, rank)
    far3 = single_far(whole3, index_x, index_y, couple3[0, 0])
    whole4 = up_level(whole3, transfer4).astype(jnp.bfloat16)
    anc_x = index_x // 2
    anc_y = index_y // 2
    far_top = top_single(whole4, anc_x, anc_y, couple_top[0, 0])
    couple_anc = lax.dynamic_index_in_dim(
        lax.dynamic_index_in_dim(couple4, anc_x, 0, keepdims=False), anc_y, 0, keepdims=False
    )
    down4 = single_far(whole4, anc_x, anc_y, couple_anc).astype(jnp.bfloat16)
    transfer_anc = lax.dynamic_index_in_dim(
        lax.dynamic_index_in_dim(transfer4, anc_x, 0, keepdims=False), anc_y, 0, keepdims=False
    )
    slot = 2 * (index_x % 2) + index_y % 2
    transfer_own = lax.dynamic_index_in_dim(transfer_anc, slot, 0, keepdims=False)
    down3 = (
        far3
        + far_top
        + jnp.einsum("kl,vl->vk", transfer_own, down4, preferred_element_type=jnp.float32)
    ).astype(jnp.bfloat16)
    down3 = down3.reshape(1, 1, nvec, rank)
    down2 = (far2 + down_level(down3, transfer3)).astype(jnp.bfloat16)
    down1 = (far1 + down_level(down2, transfer2)).astype(jnp.bfloat16)
    down0 = (far0 + down_level(down1, transfer1)).astype(jnp.bfloat16)
    near = lax.map(one_row, jnp.arange(tile, dtype=jnp.int32))
    return near + jnp.einsum(
        "ijkp,ijvk->ijvp", leaf_basis, down0, preferred_element_type=jnp.float32
    )


def solution(mesh):
    in_specs = (
        P("gx", "gy", None, None),
        P("gx", "gy", None, None),
        P("gx", "gy", None, None),
        P("gx", "gy", None, None),
        P("gx", "gy", None, None),
        P("gx", "gy", None, None),
        P("gx", "gy", None, None),
        P(),
        P("gx", "gy", None, None),
        P("gx", "gy", None, None, None),
        P("gx", "gy", None, None, None),
        P("gx", "gy", None, None, None),
        P(),
    )
    out_specs = P("gx", "gy", None, None)
    return jax.shard_map(
        on_device, mesh=mesh, in_specs=in_specs, out_specs=out_specs, check_vma=False
    )
```

profile of v0, /device:TPU:1, one launch (start us, length us, event | category | flops | bytes accessed | tf_op | source)
XLA Modules:
  0.0 1684.6 jit_solution(18020589429470841251)
XLA Ops:
  9.1 4.5 collective-permute-start.8
  14.3 2.5 collective-permute-start.9
  19.6 3.0 collective-permute-start.4
  26.0 3.6 collective-permute-start
  29.9 609.5 %all_gather.10 = bf16[256,2,2,256]{3,2,1,0:T(2,128)(2,1)S(1)} all-gather(bf16[1,2,2,256]{3,2,1,0:T(2,128)(2,1)S(1)} %reshape.318), channel_id=1, replica_groups=mesh['gx'=16,'gy'=16] {'gx','gy'}, dimensions={0}, use_global_device_ids=true | all-gather | bytes 526336 | tf_op jit(solution)/shard_map/all_gather | solution.py:187
  647.3 620.0 %all_gather.11 = bf16[256,1,1,256]{3,2,1,0:T(2,128)(2,1)S(1)} all-gather(bf16[1,1,1,256]{3,2,1,0:T(2,128)(2,1)S(1)} %reshape.333), channel_id=1, replica_groups=mesh['gx'=16,'gy'=16] {'gx','gy'}, dimensions={0}, use_global_device_ids=true | all-gather | bytes 131584 | tf_op jit(solution)/shard_map/all_gather | solution.py:188
  1268.6 4.0 fusion.187
  1345.5 6.3 reshape.305
  1351.8 4.5 reshape.304
  1356.3 6.1 reshape.303
  1362.4 4.5 reshape.302
  1366.9 2.7 reshape.315
  1374.7 22.0 %collective-permute-start.1 = (bf16[1,8,8,256]{3,2,1,0:T(8,128)(2,1)}, bf16[1,8,8,256]{3,2,1,0:T(8,128)(2,1)}, u32[]{:S(2)}, u32[]{:S(2)}) collective-permute-start(bf16[1,8,8,256]{3,2,1,0:T(8,128)(2,1)} %get-tuple-element.234), channel_id=1, source_target_pairs={{16,0},{32,16},{48,32},{64,48},{80,64},{96,80},{112,96},{128,112},... | collective-permute-start | bytes 98312 | tf_op jit(solution)/shard_map/ppermute | solution.py:15
  1399.0 5.4 collective-permute-start.6
  1407.1 5.5 collective-permute-start.10
  1415.2 3.4 collective-permute-done.11
  1431.1 3.7 collective-permute-start.2
  1437.0 4.1 collective-permute-done.3
  1441.9 220.7 %while.12 = (s32[]{:T(128)}, f32[8,8,8,256]{3,2,1,0:T(8,128)}, s32[8]{0:T(128)S(1)}, bf16[10,10,8,256]{3,2,1,0:T(8,128)(2,1)}, bf16[8,8,2,256]{3,1,2,0:T(8,128)(...) while((s32[]{:T(128)}, f32[8,8,8,256]{3,2,1,0:T(8,128)}, ...), condition=%wide.region_1.2_spmd, body=%wide.region_0.1_spmd.sunk | while | flops 133865488 | bytes 3752888 | solution.py:219
  1449.2 2.6 fusion.243
  1454.0 2.2 convolution_add_fusion.17
  1462.7 2.2 convolution_add_fusion.21
  1467.1 2.5 fusion.252
  1476.7 2.6 fusion.243
  1490.2 2.2 convolution_add_fusion.21
  1494.6 2.5 fusion.252
  1504.3 2.6 fusion.243
  1509.2 2.2 convolution_add_fusion.17
  1517.8 2.2 convolution_add_fusion.21
  1522.2 2.5 fusion.252
  1531.9 2.6 fusion.243
  1536.7 2.2 convolution_add_fusion.17
  1545.4 2.2 convolution_add_fusion.21
  1549.8 2.5 fusion.252
  1559.5 2.6 fusion.243
  1573.0 2.2 convolution_add_fusion.21
  1577.4 2.5 fusion.252
  1587.1 2.6 fusion.243
  1600.6 2.2 convolution_add_fusion.21
  1605.0 2.5 fusion.252
  1614.6 2.6 fusion.243
  1628.1 2.2 convolution_add_fusion.21
  1632.5 2.5 fusion.252
  1642.2 2.6 fusion.243
  1655.7 2.2 convolution_add_fusion.21
  1660.1 2.5 fusion.252
  1662.6 4.0 copy.520
  1666.6 4.0 reshape.310
  (672 shorter events, 235.5 us)
Async XLA Ops:
  6.5 1294.5 %copy-start = (bf16[8,8,4,32,32]{4,3,2,1,0:T(8,128)(2,1)S(1)}, bf16[8,8,4,32,32]{4,3,2,1,0:T(8,128)(2,1)}, u32[]{:S(2)}) copy-start(bf16[8,8,4,32,32]{4,3,2,1,0:T(8,128)(2,1)} %param.27) | copy-start | bytes 1572868
  6.5 12.4 copy-start.25
  6.5 23.1 %copy-start.20 = (bf16[2,2,4,32,32]{4,3,2,1,0:T(8,128)(2,1)S(1)}, bf16[2,2,4,32,32]{4,3,2,1,0:T(8,128)(2,1)}, u32[]{:S(2)}) copy-start(bf16[2,2,4,32,32]{4,3,2,1,0:T(8,128)(2,1)} %param.25) | copy-start | bytes 98308
  6.5 1656.1 %all-gather.2.cloned.1.call-start = ((), (), s32[]{:S(2)}) async-start(), calls=%async_computation | async-start | bytes 2105344 | tf_op jit(solution)/shard_map/all_gather | solution.py:186
  9.1 1395.3 %collective-permute-start.8 = (bf16[2,8,256]{2,1,0:T(8,128)(2,1)}, bf16[2,8,256]{2,1,0:T(8,128)(2,1)}, u32[]{:S(2)}, u32[]{:S(2)}) collective-permute-start(bf16[2,8,256]{2,1,0:T(8,128)(2,1)} %slice.1281), channel_id=1, source_target_pairs={{0,16},{16,32},{32,48},{48,64},{64,80},{80,96},{96,112},{112,128},... | collective-permute-start | bytes 24584 | tf_op jit(solution)/shard_map/ppermute | solution.py:14
  14.3 1392.1 %collective-permute-start.9 = (bf16[2,8,256]{2,1,0:T(8,128)(2,1)}, bf16[2,8,256]{2,1,0:T(8,128)(2,1)}, u32[]{:S(2)}, u32[]{:S(2)}) collective-permute-start(bf16[2,8,256]{2,1,0:T(8,128)(2,1)} %slice.1283), channel_id=1, source_target_pairs={{16,0},{32,16},{48,32},{64,48},{80,64},{96,80},{112,96},{128,112},... | collective-permute-start | bytes 24584 | tf_op jit(solution)/shard_map/ppermute | solution.py:15
  18.9 620.5 %copy-start.27 = (bf16[8,8,2,256]{3,1,2,0:T(8,128)(2,1)}, bf16[8,8,2,256]{3,1,2,0:T(8,128)(2,1)S(1)}, u32[]{:S(2)}) copy-start(bf16[8,8,2,256]{3,1,2,0:T(8,128)(2,1)S(1)} %copy.422) | copy-start | bytes 196612
  19.6 1355.2 %collective-permute-start.4 = (bf16[1,8,2,256]{3,1,2,0:T(8,128)(2,1)}, bf16[1,8,2,256]{3,1,2,0:T(8,128)(2,1)}, u32[]{:S(2)}, u32[]{:S(2)}) collective-permute-start(bf16[1,8,2,256]{3,1,2,0:T(8,128)(2,1)} %get-tuple-element.319), channel_id=1, source_target_pairs={{0,16},{16,32},{32,48},{48,64},{64,80},{80,96},{96,112},{112,128},... | collective-permute-start | bytes 24584 | tf_op jit(solution)/shard_map/ppermute | solution.py:14
  22.6 1375.6 %collective-permute-start.5 = (bf16[1,8,2,256]{3,1,2,0:T(8,128)(2,1)}, bf16[1,8,2,256]{3,1,2,0:T(8,128)(2,1)}, u32[]{:S(2)}, u32[]{:S(2)}) collective-permute-start(bf16[1,8,2,256]{3,1,2,0:T(8,128)(2,1)} %get-tuple-element.318), channel_id=1, source_target_pairs={{16,0},{32,16},{48,32},{64,48},{80,64},{96,80},{112,96},{128,112},... | collective-permute-start | bytes 24584 | tf_op jit(solution)/shard_map/ppermute | solution.py:15
  26.0 1403.6 %collective-permute-start = (bf16[1,8,8,256]{3,2,1,0:T(8,128)(2,1)}, bf16[1,8,8,256]{3,2,1,0:T(8,128)(2,1)}, u32[]{:S(2)}, u32[]{:S(2)}) collective-permute-start(bf16[1,8,8,256]{3,2,1,0:T(8,128)(2,1)} %get-tuple-element.235), channel_id=1, source_target_pairs={{0,16},{16,32},{32,48},{48,64},{64,80},{80,96},{96,112},{112,128},... | collective-permute-start | bytes 98312 | tf_op jit(solution)/shard_map/ppermute | solution.py:14
  29.6 617.4 %copy-start.35 = (bf16[1,1,4,32,32]{4,3,2,1,0:T(8,128)(2,1)S(1)}, bf16[1,1,4,32,32]{4,3,2,1,0:T(8,128)(2,1)}, u32[]{:S(2)}) copy-start(bf16[1,1,4,32,32]{4,3,2,1,0:T(8,128)(2,1)} %param.26) | copy-start | bytes 24580
  640.3 6.9 copy-start.18
  645.5 1.7 copy-start.28
  645.5 1.7 copy-start.33
  1268.6 4.1 copy-start.15
  1268.6 4.9 copy-start.19
  1272.6 16.7 copy-start.29
  1304.1 2.7 copy-start.32
  1313.1 3.5 copy-start.17
  1313.1 3.5 copy-start.31
  1337.1 7.3 copy-start.21
  1345.5 6.3 copy-start.7
  1356.3 6.1 copy-start.6
  1362.4 7.2 copy-start.14
  1366.9 6.4 copy-start.13
  1369.6 4.5 copy-start.24
  1374.7 55.6 %collective-permute-start.1 = (bf16[1,8,8,256]{3,2,1,0:T(8,128)(2,1)}, bf16[1,8,8,256]{3,2,1,0:T(8,128)(2,1)}, u32[]{:S(2)}, u32[]{:S(2)}) collective-permute-start(bf16[1,8,8,256]{3,2,1,0:T(8,128)(2,1)} %get-tuple-element.234), channel_id=1, source_target_pairs={{16,0},{32,16},{48,32},{64,48},{80,64},{96,80},{112,96},{128,112},... | collective-permute-start | bytes 98312 | tf_op jit(solution)/shard_map/ppermute | solution.py:15
  1399.0 13.6 collective-permute-start.6
  1404.4 10.1 collective-permute-start.7
  1407.1 8.1 collective-permute-start.10
  1412.6 5.9 collective-permute-start.11
  1419.7 2.2 copy-start.4
  1421.9 2.2 copy-start.3
  1424.0 2.2 copy-start.2
  1426.2 2.2 copy-start.1
  1428.4 1.9 copy-start.12
  1431.1 5.9 collective-permute-start.2
  1434.9 6.3 collective-permute-start.3
  1449.1 2.6 copy-start.23
  1476.7 2.6 copy-start.23
  1504.3 2.6 copy-start.23
  1531.9 2.6 copy-start.23
  1559.5 2.6 copy-start.23
  1587.1 2.6 copy-start.23
  1614.6 2.6 copy-start.23
  1642.2 2.6 copy-start.23
  1671.9 1.7 copy-start.8
  1673.6 1.7 copy-start.22
  (8 other events, 9.4 us)
Sparse Core Ops, SparseCore 0:
  19.0 707.0 all-gather.1
where the time goes:
time: 1690 us; the launch traced here: 1680 us
  blocking collectives  1230 us (73%)
  matrix products  189 us (11%)
  local copies, waits for them, and re-layouts  136 us (8%)
  starting transfers between devices  56.7 us (3%)
  loops' own time  45.2 us (3%)
    all_gather x1, blocking collectives, on_device(): lax.all_gather(flat3, ('gx', 'gy'), axis=0, tiled=True)  620 us
    all_gather x1, blocking collectives, on_device(): lax.all_gather(flat2, ('gx', 'gy'), axis=0, tiled=True)  610 us
    dot_general x72, matrix products, one_row(): jnp.einsum('tpq,tvq->tvp', kern, src_vec[b:b + tile], preferred_element_t...  163 us
    unnamed x390, local copies, waits for them, and re-layouts  54.9 us
    another operation x1, loops' own time, on_device(): near = lax.map(one_row, jnp.arange(tile, dtype=jnp.int32))  45.2 us
  transfers between devices with their start and end apart: 13, of which 2 were waited for; matrix products, arithmetic and copies ran while one was open for 18% of the time, Pallas kernels for 0%

commit v1 on v0

v1 whole, which is shorter than its diff:
```python
import functools

import jax
import jax.numpy as jnp
from jax import lax
from jax.experimental import pallas as pl
from jax.experimental.pallas import tpu as pltpu
from jax.sharding import PartitionSpec as P

BF = jnp.bfloat16
F32 = jnp.float32
MESH = pl.DeviceIdType.MESH
ROOT3 = 1.7320508075688772
LOG2E = 1.4426950408889634
NX = 16
NY = 16
SIDES = [(a, b) for a in (-1, 0, 1) for b in (-1, 0, 1) if (a, b) != (0, 0)]


def dot_t(a, b):
    return lax.dot_general(a, b, (((1,), (1,)), ((), ())), preferred_element_type=F32)


def dot_n(a, b):
    return jnp.dot(a, b, preferred_element_type=F32)


def lane(shape):
    return lax.broadcasted_iota(jnp.int32, shape, 1)


def rounded(x):
    return x.astype(BF).astype(F32)


def diagonal(o):
    group = lane((8, 128)) // 32
    out = o[0:8]
    for s in range(1, 4):
        out = jnp.where(group == s, o[8 * s : 8 * s + 8], out)
    return out


def set_columns(npk, colb, hi, hj):
    rows = npk[hi, hj].astype(F32)[8:16]
    cols = rows.T
    for c in range(4):
        colb[c] = jnp.broadcast_to(cols[:, c : c + 1], (256, 128)).astype(BF)


def kernel_tile(npk, colb, yi, yj, step_x, step_y):
    row_x = npk[yi, yj, 9:10] if step_x == -1 else npk[yi, yj, 8:9]
    row_y = npk[yi, yj, 11:12] if step_y == -1 else npk[yi, yj, 10:11]
    col_x = 1 if step_x == 1 else 0
    col_y = 3 if step_y == 1 else 2
    halves = []
    for h in range(2):
        dx = row_x[:, 128 * h : 128 * h + 128] - colb[col_x]
        dy = row_y[:, 128 * h : 128 * h + 128] - colb[col_y]
        r2 = jnp.maximum(dx * dx + dy * dy, jnp.asarray(1e-30, BF))
        r = r2 * lax.rsqrt(r2)
        e = jnp.exp2(r * jnp.asarray(-ROOT3 * LOG2E, BF))
        halves.append((r + jnp.asarray(1.0 / ROOT3, BF)) * e)
    return jnp.concatenate(halves, axis=1)


def near_box(npk, acc, colb, i, j, forward, one_way, own=True):
    set_columns(npk, colb, i + 1, j + 1)
    mine = npk[i + 1, j + 1][0:8] if False else npk[i + 1, j + 1].astype(F32)[0:8].astype(BF)
    total = None
    if own:
        tile = kernel_tile(npk, colb, i + 1, j + 1, 0, 0)
        total = dot_t(mine, tile)
    for a, b in forward:
        tile = kernel_tile(npk, colb, i + 1 + a, j + 1 + b, a, b)
        other = npk[i + 1 + a, j + 1 + b].astype(F32)[0:8].astype(BF)
        part = dot_t(other, tile)
        total = part if total is None else total + part
        acc[i + a, j + b] += dot_n(mine, tile)
    for a, b in one_way:
        tile = kernel_tile(npk, colb, i + 1 + a, j + 1 + b, a, b)
        other = npk[i + 1 + a, j + 1 + b].astype(F32)[0:8].astype(BF)
        part = dot_t(other, tile)
        total = part if total is None else total + part
    acc[i, j] += total


def near_inside(npk, acc, colb):
    acc[...] = jnp.zeros(acc.shape, F32)

    def middle(n, _):
        i, j = n // 6, n % 6 + 1
        near_box(npk, acc, colb, i, j, [(0, 1), (1, -1), (1, 0), (1, 1)], [])
        return 0

    lax.fori_loop(0, 42, middle, 0)

    def ends(i, _):
        near_box(npk, acc, colb, i, 0, [(0, 1), (1, 0), (1, 1)], [])
        near_box(npk, acc, colb, i, 7, [(1, -1), (1, 0)], [])
        return 0

    lax.fori_loop(0, 7, ends, 0)

    def bottom(j, _):
        near_box(npk, acc, colb, 7, j, [(0, 1)], [])
        return 0

    lax.fori_loop(0, 7, bottom, 0)
    near_box(npk, acc, colb, 7, 7, [], [])


def near_edges(npk, acc, colb):
    def rows(j, _):
        near_box(npk, acc, colb, 0, j, [], [(-1, -1), (-1, 0), (-1, 1)], own=False)
        near_box(npk, acc, colb, 7, j, [], [(1, -1), (1, 0), (1, 1)], own=False)
        return 0

    lax.fori_loop(0, 8, rows, 0)

    def cols(i, _):
        near_box(npk, acc, colb, i, 0, [], [(-1, -1), (0, -1), (1, -1)], own=False)
        near_box(npk, acc, colb, i, 7, [], [(-1, 1), (0, 1), (1, 1)], own=False)
        return 0

    lax.fori_loop(1, 7, cols, 0)
    near_box(npk, acc, colb, 0, 0, [], [(0, -1), (1, -1)], own=False)
    near_box(npk, acc, colb, 7, 0, [], [(-1, -1), (0, -1)], own=False)
    near_box(npk, acc, colb, 0, 7, [], [(0, 1), (1, 1)], own=False)
    near_box(npk, acc, colb, 7, 7, [], [(-1, 1), (0, 1)], own=False)


def own_coefficients(vec, basis, i):
    parts = []
    for h in range(2):
        v4 = vec[i, 4 * h : 4 * h + 4].astype(F32).reshape(32, 256).astype(BF)
        b4 = basis[i, 4 * h : 4 * h + 4].reshape(128, 256)
        parts.append(diagonal(dot_t(v4, b4)))
    return rounded(jnp.concatenate(parts, axis=1))


def join_pair(upper, lower, n):
    t = 128 * (n // 2)
    u, w = upper[:, t : t + 128], lower[:, t : t + 128]
    low = lane((8, 128)) < 64
    if n % 2 == 0:
        return jnp.where(low, u, pltpu.roll(w, 64, 1))
    return jnp.where(low, pltpu.roll(u, 64, 1), w)


def row_up(upper, lower, transfer, m, count):
    parts = []
    for n in range(count):
        both = join_pair(upper, lower, n).astype(BF)
        parts.append(dot_n(both, transfer[m, n].reshape(128, 32)))
    return rounded(jnp.concatenate(parts, axis=1))


def shifted(row):
    return pltpu.roll(row, row.shape[1] - 64, 1)


def class_pieces(par_x, par_y):
    pieces = []
    for a in range(6):
        if abs(a - 2 - par_x) <= 1:
            if par_y == 0:
                pieces += [(a, 0, 32), (a, 128, 192)]
            else:
                pieces += [(a, 0, 64), (a, 160, 192)]
        else:
            pieces += [(a, 0, 192)]
    return pieces


def class_stack(window, par_x, par_y):
    return jnp.concatenate([window[a][:, lo:hi] for a, lo, hi in class_pieces(par_x, par_y)], axis=1)


def far_parent(window, couple4):
    stacks = [class_stack(window, px, py) for px in range(2) for py in range(2)]
    return diagonal(dot_t(jnp.concatenate(stacks, axis=0).astype(BF), couple4))


def four(ref, m, n):
    return ref[2 * m : 2 * m + 2, 2 * n : 2 * n + 2].reshape(4 * ref.shape[2], ref.shape[3])


def far_single(window, couple, bit_x, bit_y):
    stacks = [class_stack(window, px, py) for px in range(2) for py in range(2)]
    first = jnp.where(bit_y == 0, stacks[0], stacks[1])
    second = jnp.where(bit_y == 0, stacks[2], stacks[3])
    return dot_t(jnp.where(bit_x == 0, first, second).astype(BF), couple)


def single_window(read, size, width, box_x, box_y):
    half_x, half_y = box_x // 2, box_y // 2
    start = 64 * half_y - 64
    lanes = lane((8, width))
    column = lanes + start
    rows = []
    for a in range(6):
        r = 2 * half_x - 2 + a
        row = read(jnp.clip(r, 0, size - 1))
        row = pltpu.roll(row, lax.rem(2 * width - start, width), 1)
        keep = (column >= 0) & (column < width) & (r >= 0) & (r < size)
        rows.append(jnp.where(keep, row, 0.0))
    return rows


def slot_part(x, s):
    if s:
        x = pltpu.roll(x, 128 - 32 * s, 1)
    return x[:, :32]


def spread(x, transfer):
    return dot_t(x.astype(BF), transfer.reshape(128, 32))


def send_kernel(off, vec, basis, tr1, tr2, tr3, npk_out, d0_out, e_out, w3_out, npk, d0, e, g1, g2, send, recv, send1, recv1, send2, recv2):
    gx, gy = lax.axis_index("gx"), lax.axis_index("gy")

    def there(a, b):
        x, y = gx + a, gy + b
        ok = None
        for test in ([x >= 0] if a < 0 else []) + ([x < NX] if a > 0 else []) + ([y >= 0] if b < 0 else []) + ([y < NY] if b > 0 else []):
            ok = test if ok is None else ok & test
        return ok, x, y

    npk[...] = jnp.zeros(npk.shape, BF)
    d0[...] = jnp.zeros(d0.shape, BF)
    e[...] = jnp.zeros(e.shape, BF)

    barrier = pltpu.get_barrier_semaphore()
    for k in range(1, NX):
        pl.semaphore_signal(barrier, inc=1, device_id=(lax.rem(gx + k, NX), gy), device_id_type=MESH)
    for k in range(1, NY):
        pl.semaphore_signal(barrier, inc=1, device_id=(gx, lax.rem(gy + k, NY)), device_id_type=MESH)
    for a, b in SIDES:
        if a and b:
            ok, x, y = there(a, b)

            @pl.when(ok)
            def _():
                pl.semaphore_signal(barrier, inc=1, device_id=(x, y), device_id_type=MESH)

    def pack(i, _):
        for j in range(8):
            o = off[i, j].astype(F32)
            v = vec[i, j].astype(F32)
            x, y = o[0:1], o[1:2]
            npk[i + 1, j + 1] = jnp.concatenate([v, x, x - 1.0, y, y - 1.0, jnp.zeros((4, 256), F32)], axis=0).astype(BF)
        return 0

    lax.fori_loop(0, 8, pack, 0)

    c0 = [own_coefficients(vec, basis, i) for i in range(8)]
    for m in range(4):
        d0[1 + m, :, 128:384] = jnp.concatenate([c0[2 * m], c0[2 * m + 1]], axis=0).astype(BF)
    c1 = [row_up(c0[2 * m], c0[2 * m + 1], tr1, m, 4) for m in range(4)]
    e[2, :, 128:256] = jnp.concatenate([c1[0], c1[1]], axis=0).astype(BF)
    e[4, :, 128:256] = jnp.concatenate([c1[2], c1[3]], axis=0).astype(BF)
    blank = jnp.zeros((8, 64), F32)
    c2 = [jnp.concatenate([row_up(c1[2 * m], c1[2 * m + 1], tr2, m, 2), blank], axis=1) for m in range(2)]
    e[3, :, 128:256] = jnp.concatenate([c2[0], c2[1]], axis=0).astype(BF)
    c3 = row_up(c2[0], c2[1], tr3, 0, 1)
    mine = jnp.concatenate([c3] * 4, axis=1)
    g1[gy] = jnp.where(lane((8, 128)) // 32 == lax.rem(gy, 4), mine, 0.0)

    beside_x = (gx > 0).astype(jnp.int32) + (gx < NX - 1).astype(jnp.int32)
    beside_y = (gy > 0).astype(jnp.int32) + (gy < NY - 1).astype(jnp.int32)
    pl.semaphore_wait(barrier, NX - 1 + NY - 1 + beside_x * beside_y)

    def row_copy(k):
        other = lax.rem(gy + k, NY)
        return pltpu.make_async_remote_copy(
            src_ref=g1.at[gy], dst_ref=g1.at[gy], send_sem=send1.at[k], recv_sem=recv1.at[NY - k],
            device_id=(gx, other), device_id_type=MESH,
        )

    def col_copy(k):
        other = lax.rem(gx + k, NX)
        return pltpu.make_async_remote_copy(
            src_ref=g2.at[gx], dst_ref=g2.at[gx], send_sem=send2.at[k], recv_sem=recv2.at[NX - k],
            device_id=(other, gy), device_id_type=MESH,
        )

    for k in range(1, NY):
        row_copy(k).start()

    def side_copies(a, b):
        ok, x, y = there(a, b)
        n = SIDES.index((a, b))

        def part(step, low, high, count):
            return {0: (low, low, count), 1: (high[0], high[1], high[2]), -1: (low, count + low, high[2])}[step]

        rows = {0: (1, 1, 8), 1: (8, 0, 1), -1: (1, 9, 1)}
        r0 = {0: (1, 1, 4), 1: (4, 0, 1), -1: (1, 5, 1)}[a]
        l0 = {0: (128, 128, 256), 1: (256, 0, 128), -1: (128, 384, 128)}[b]
        r1 = {0: (2, 2, 3), 1: (3, 0, 2), -1: (2, 5, 2)}[a]
        l1 = {0: (128, 128, 128), 1: (128, 0, 128), -1: (128, 256, 128)}[b]
        ra, rb = rows[a], rows[b]

        def remote(src, dst, t):
            return pltpu.make_async_remote_copy(
                src_ref=src, dst_ref=dst, send_sem=send.at[n, t], recv_sem=recv.at[n, t],
                device_id=(x, y), device_id_type=MESH,
            )

        return ok, [
            remote(d0.at[pl.ds(r0[0], r0[2]), :, pl.ds(l0[0], l0[2])], d0.at[pl.ds(r0[1], r0[2]), :, pl.ds(l0[1], l0[2])], 0),
            remote(e.at[pl.ds(r1[0], r1[2]), :, pl.ds(l1[0], l1[2])], e.at[pl.ds(r1[1], r1[2]), :, pl.ds(l1[1], l1[2])], 1),
            remote(npk.at[pl.ds(ra[0], ra[2]), pl.ds(rb[0], rb[2])], npk.at[pl.ds(ra[1], ra[2]), pl.ds(rb[1], rb[2])], 2),
        ]

    for a, b in SIDES:
        ok, copies = side_copies(a, b)

        @pl.when(ok)
        def _():
            for c in copies:
                c.start()

    for k in range(1, NY):
        row_copy(k).wait_recv()
    groups = [g1[4 * t] + g1[4 * t + 1] + g1[4 * t + 2] + g1[4 * t + 3] for t in range(4)]
    g2[gx] = jnp.concatenate(
        [jnp.concatenate(groups[0:2], axis=1), jnp.concatenate(groups[2:4], axis=1)], axis=0
    ).astype(BF)
    for k in range(1, NX):
        col_copy(k).start()

    for a, b in SIDES:
        copies = side_copies(a, b)[1]

        @pl.when(there(-a, -b)[0])
        def _():
            for c in copies:
                c.wait_recv()

    npk_out[...] = npk[...]
    d0_out[...] = d0[...]
    e_out[...] = e[...]
    for k in range(1, NX):
        col_copy(k).wait_recv()
    w3_out[...] = g2[...]
    for a, b in SIDES:
        ok, copies = side_copies(a, b)

        @pl.when(ok)
        def _():
            for c in copies:
                c.wait_send()

    for k in range(1, NY):
        row_copy(k).wait_send()
    for k in range(1, NX):
        col_copy(k).wait_send()


def rest_kernel(npk, d0, e, w3, basis, cp0, cp1, cp2, cp3, cp4, cpt, tr1, tr2, tr3, tr4, out, acc, colb):
    gx, gy = lax.axis_index("gx"), lax.axis_index("gy")
    near_inside(npk, acc, colb)
    near_edges(npk, acc, colb)

    whole3 = w3[...].astype(F32)
    rows3 = [jnp.concatenate([whole3[i, 0:8], whole3[i, 8:16]], axis=1) for i in range(NX)]
    rows4 = [row_up(rows3[2 * m], rows3[2 * m + 1], tr4, m, NY // 2) for m in range(NX // 2)]

    def select(rows, r):
        got = rows[0]
        for t in range(1, len(rows)):
            got = jnp.where(r == t, rows[t], got)
        return got

    def read3(r):
        block = w3[r].astype(F32)
        return jnp.concatenate([block[0:8], block[8:16]], axis=1)

    anc_x, anc_y = gx // 2, gy // 2
    far3 = far_single(single_window(read3, NX, 32 * NY, gx, gy), cp3[0, 0], gx % 2, gy % 2)
    window4 = single_window(lambda r: select(rows4, r), NX // 2, 16 * NY, anc_x, anc_y)
    down4 = far_single(window4, cp4[anc_x, anc_y], anc_x % 2, anc_y % 2)
    base_x, base_y = 2 * (anc_x // 2), 2 * (anc_y // 2)
    box_y = lane((8, 16 * NY)) // 32
    near_y = (box_y >= base_y - 2) & (box_y <= base_y + 3)
    masked = []
    for m in range(NX // 2):
        near_x = (m >= base_x - 2) & (m <= base_x + 3)
        masked.append(jnp.where(near_y & near_x, 0.0, rows4[m]))
    top = dot_t(jnp.concatenate(masked, axis=1).astype(BF), cpt[0, 0])
    slot = 2 * (gx % 2) + gy % 2
    own4 = dot_t(down4.astype(BF), tr4[anc_x, anc_y, slot])
    down3 = far3 + top + own4

    tiles = [e[t].astype(F32) for t in (1 - 1, 3, 6)]
    tiles = [e[0].astype(F32), e[3].astype(F32), e[6].astype(F32)]
    window = []
    for t in tiles:
        wide = jnp.concatenate([t[:, 0:64], t[:, 128:192], t[:, 256:320]], axis=1)
        window += [wide[0:8], wide[8:16]]
    down2 = far_parent(window, four(cp2, 0, 0)) + spread(down3, tr3[0, 0])

    rows = []
    for t in (1, 2, 4, 5):
        block = e[t].astype(F32)
        rows += [block[0:8], block[8:16]]
    moved = [shifted(row) for row in rows]
    down1 = {}
    for m in range(2):
        for n in range(2):
            window = []
            for a in range(6):
                at = 64 + 64 * n
                window.append(rows[2 * m + a][:, at : at + 256] if at % 128 == 0 else moved[2 * m + a][:, at - 64 : at + 192])
            far = far_parent(window, four(cp1, m, n))
            down1[m, n] = far + spread(slot_part(down2, 2 * m + n), tr2[m, n])

    rows = []
    for t in range(6):
        block = d0[t].astype(F32)
        rows += [block[0:8], block[8:16]]
    moved = [shifted(row) for row in rows]
    group = lane((8, 128)) // 32
    for m in range(4):
        for n in range(4):
            window = []
            for a in range(6):
                at = 64 + 64 * n
                window.append(rows[2 * m + a][:, at : at + 256] if at % 128 == 0 else moved[2 * m + a][:, at - 64 : at + 192])
            far = far_parent(window, four(cp0, m, n))
            s = 2 * (m % 2) + n % 2
            down0 = far + spread(slot_part(down1[m // 2, n // 2], s), tr1[m, n])
            parts = jnp.concatenate([jnp.where(group == t, down0, 0.0) for t in range(4)], axis=0).astype(BF)
            given = dot_n(parts, four(basis, m, n))
            for t in range(4):
                i, j = 2 * m + t // 2, 2 * n + t % 2
                out[i, j] = acc[i, j] * (0.0625 * ROOT3) + given[8 * t : 8 * t + 8]


def on_device(off, vec, basis, cp0, cp1, cp2, cp3, cp4, cpt, tr1, tr2, tr3, tr4):
    vmem = pl.BlockSpec(memory_space=pltpu.VMEM)
    sem = pltpu.SemaphoreType.DMA
    shapes = [(10, 10, 16, 256), (6, 16, 512), (7, 16, 384), (NX, 16, 256)]
    npk, d0, e, w3 = pl.pallas_call(
        send_kernel,
        out_shape=[jax.ShapeDtypeStruct(s, BF) for s in shapes],
        in_specs=[vmem] * 6,
        out_specs=[vmem] * 4,
        scratch_shapes=[
            pltpu.VMEM(shapes[0], BF),
            pltpu.VMEM(shapes[1], BF),
            pltpu.VMEM(shapes[2], BF),
            pltpu.VMEM((NY, 8, 128), F32),
            pltpu.VMEM(shapes[3], BF),
            sem((8, 3)),
            sem((8, 3)),
            sem((NY,)),
            sem((NY,)),
            sem((NX,)),
            sem((NX,)),
        ],
        compiler_params=pltpu.CompilerParams(collective_id=0, has_side_effects=True, vmem_limit_bytes=24 << 20),
        name="coefficients",
    )(off, vec, basis, tr1, tr2, tr3)
    return pl.pallas_call(
        rest_kernel,
        out_shape=jax.ShapeDtypeStruct((8, 8, 8, 256), F32),
        in_specs=[vmem] * 15,
        out_specs=vmem,
        scratch_shapes=[pltpu.VMEM((8, 8, 8, 256), F32), pltpu.VMEM((4, 256, 128), BF)],
        compiler_params=pltpu.CompilerParams(vmem_limit_bytes=48 << 20),
        name="fields",
    )(npk, d0, e, w3, basis, cp0, cp1, cp2, cp3, cp4, cpt, tr1, tr2, tr3, tr4)


def solution(mesh):
    tiled = P("gx", "gy", None, None)
    tiled5 = P("gx", "gy", None, None, None)
    in_specs = (tiled,) * 7 + (P(), tiled) + (tiled5,) * 3 + (P(),)
    return jax.shard_map(on_device, mesh=mesh, in_specs=in_specs, out_specs=tiled, check_vma=False)
```

time: 1690 us -> 96.9 us (0.06)
  blocking collectives: 1230 us -> 0 us
  matrix products: 189 us -> 0 us
  local copies, waits for them, and re-layouts: 136 us -> 13.5 us
  Pallas kernels: 0 us -> 82.8 us
  starting transfers between devices: 56.7 us -> 0 us
  loops' own time: 45.2 us -> 0 us
    all_gather x2 -> x0, blocking collectives: 1230 us -> none  [the longest x1 620 us: on_device(): lax.all_gather(flat3, ('gx', 'gy'), axis=0, tiled=True)]
    dot_general x102 -> x0, matrix products: 189 us -> none  [the longest x72 163 us: one_row(): jnp.einsum('tpq,tvq->tvp', kern, src_vec[b:b + tile], preferred_element_t...]
    pallas_call x0 -> x2, Pallas kernels: none -> 82.8 us  [the longest x1 58.5 us: on_device(): pl.pallas_call(rest_kernel, out_shape=jax.ShapeDtypeStruct((8, 8, 8, 256)...]
    ppermute x12 -> x0, starting transfers between devices: 56.7 us -> none  [the longest x6 30.9 us: with_halo(): after = lax.ppermute(first, axis, down)]
    another operation x1 -> x0, loops' own time: 45.2 us -> none  [on_device(): near = lax.map(one_row, jnp.arange(tile, dtype=jnp.int32))]
    unnamed x390 -> x28, local copies, waits for them, and re-layouts: 54.9 us -> 13.5 us
    reshape x18 -> x0, local copies, waits for them, and re-layouts: 34.4 us -> none  [the longest x8 28.6 us: far_level(): part = couple[par_x::2, par_y::2].reshape(half_x, half_y, rank, 27, rank)]
  transfers between devices with their start and end apart: 13 -> 0, of which waited for: 2 -> 0; matrix products, arithmetic and copies ran while one was open for 18% -> 0% of each run, Pallas kernels for 0% -> 0%
where the time goes in v1:
time: 96.9 us; the launch traced here: 96.3 us
  Pallas kernels  82.8 us (85%)
  local copies, waits for them, and re-layouts  13.5 us (14%)
    pallas_call x1, Pallas kernels, on_device(): pl.pallas_call(rest_kernel, out_shape=jax.ShapeDtypeStruct((8, 8, 8, 256)...  58.5 us
    pallas_call x1, Pallas kernels, on_device(): pl.pallas_call(send_kernel, out_shape=[jax.ShapeDtypeStruct(s, BF) for s...  24.3 us
    unnamed x28, local copies, waits for them, and re-layouts  13.5 us

profile of v1, /device:TPU:1, one launch (start us, length us, event | category | flops | bytes accessed | tf_op | source)
XLA Modules:
  0.0 96.3 jit_solution(583124373797876192)
XLA Ops:
  0.0 0.0 copy-start
  0.0 1.2 %copy-done = bf16[8,8,32,256]{3,2,1,0:T(8,128)(2,1)S(1)} copy-done((bf16[8,8,32,256]{3,2,1,0:T(8,128)(2,1)S(1)}, bf16[8,8,32,256]{3,2,1,0:T(8,128)(2,1)}, u32[]{:S(2)}) %copy-start) | copy-done | bytes 1048600
  1.2 0.0 copy-start.2
  1.2 1.0 %copy-done.2 = bf16[4,4,4,32,32]{4,3,2,1,0:T(8,128)(2,1)S(1)} copy-done((bf16[4,4,4,32,32]{4,3,2,1,0:T(8,128)(2,1)S(1)}, bf16[4,4,4,32,32]{4,3,2,1,0:T(8,128)(2,1)}, u32[]{:S(2)}) %copy-start.2) | copy-done | bytes 131096
  2.3 0.0 copy-start.5
  2.3 0.9 copy-done.5
  3.2 0.0 copy-start.7
  3.2 0.9 copy-done.7
  4.1 0.0 copy-start.10
  4.1 0.8 copy-done.10
  4.9 0.0 copy-start.12
  4.9 0.8 copy-done.12
  5.7 24.3 %coefficients.1 = (bf16[10,10,16,256]{3,2,1,0:T(8,128)(2,1)S(1)}, bf16[6,16,512]{2,1,0:T(8,128)(2,1)S(1)}, bf16[7,16,384]{2,1,0:T(8,128)(2,1)S(1)}, bf16[16,16,256]{2,1,0:T(8,128)(2,1)S(1)}) custom-call(bf16[8,8,2,256]{3,2,1,0:T(2,128)(2,1)S(1)} %copy-done.12, bf16[8,8,8,256]{3,2,1,0:T(8,128)(2,1)S(1)} %copy-done.7, bf16[8,8,32,256]{3,2,1,0:T(8,128)(2,1)S(1)} %copy-done, ...), custom_call_target="tpu_custom_call" | custom-call | tf_op jit(solution)/shard_map/coefficients/pallas_call | solution.py:447
  30.0 0.0 copy-start.1
  30.0 1.2 %copy-done.1 = bf16[8,8,32,256]{3,2,1,0:T(8,128)(2,1)S(1)} copy-done((bf16[8,8,32,256]{3,2,1,0:T(8,128)(2,1)S(1)}, bf16[8,8,32,256]{3,2,1,0:T(8,128)(2,1)}, u32[]{:S(2)}) %copy-start.1) | copy-done | bytes 1048600
  31.3 0.0 copy-start.3
  31.3 1.0 %copy-done.3 = bf16[4,4,4,32,32]{4,3,2,1,0:T(8,128)(2,1)S(1)} copy-done((bf16[4,4,4,32,32]{4,3,2,1,0:T(8,128)(2,1)S(1)}, bf16[4,4,4,32,32]{4,3,2,1,0:T(8,128)(2,1)}, u32[]{:S(2)}) %copy-start.3) | copy-done | bytes 131096
  32.3 0.0 copy-start.4
  32.3 1.2 %copy-done.4 = bf16[4,4,32,864]{3,2,1,0:T(8,128)(2,1)S(1)} copy-done((bf16[4,4,32,864]{3,2,1,0:T(8,128)(2,1)S(1)}, bf16[4,4,32,864]{3,2,1,0:T(8,128)(2,1)}, u32[]{:S(2)}) %copy-start.4) | copy-done | bytes 884760
  33.5 0.0 copy-start.6
  33.5 0.9 copy-done.6
  34.4 0.0 copy-start.8
  34.4 0.9 copy-done.8
  35.3 0.0 copy-start.9
  35.3 0.9 copy-done.9
  36.2 0.0 copy-start.11
  36.2 0.8 copy-done.11
  37.0 0.0 copy-start.13
  37.0 0.8 copy-done.13
  37.8 58.5 %fields.1 = f32[8,8,8,256]{3,2,1,0:T(8,128)} custom-call(bf16[10,10,16,256]{3,2,1,0:T(8,128)(2,1)S(1)} %get-tuple-element.9.npk, bf16[6,16,512]{2,1,0:T(8,128)(2,1)S(1)} %get-tuple-element.10.d0, bf16[7,16,384]{2,1,0:T(8,128)(2,1)S(1)} %get-tuple-element.11.e, bf16[16,16,256]{2,1,0:T(8,128)(2,1)S(1)} %get-tuple-element.12.w3, ...), custom_call_target="tpu_custom_call" | custom-call | tf_op jit(solution)/shard_map/fields/pallas_call | solution.py:468
Async XLA Ops:
  0.0 1.2 %copy-start = (bf16[8,8,32,256]{3,2,1,0:T(8,128)(2,1)S(1)}, bf16[8,8,32,256]{3,2,1,0:T(8,128)(2,1)}, u32[]{:S(2)}) copy-start(bf16[8,8,32,256]{3,2,1,0:T(8,128)(2,1)} %basis.3) | copy-start | bytes 3145732
  1.2 1.0 %copy-start.2 = (bf16[4,4,4,32,32]{4,3,2,1,0:T(8,128)(2,1)S(1)}, bf16[4,4,4,32,32]{4,3,2,1,0:T(8,128)(2,1)}, u32[]{:S(2)}) copy-start(bf16[4,4,4,32,32]{4,3,2,1,0:T(8,128)(2,1)} %tr1.3) | copy-start | bytes 393220
  2.3 0.9 copy-start.5
  3.2 0.9 copy-start.7
  4.1 0.8 copy-start.10
  4.9 0.8 copy-start.12
  30.0 1.2 %copy-start.1 = (bf16[8,8,32,256]{3,2,1,0:T(8,128)(2,1)S(1)}, bf16[8,8,32,256]{3,2,1,0:T(8,128)(2,1)}, u32[]{:S(2)}) copy-start(bf16[8,8,32,256]{3,2,1,0:T(8,128)(2,1)} %basis.3) | copy-start | bytes 3145732
  31.3 1.0 %copy-start.3 = (bf16[4,4,4,32,32]{4,3,2,1,0:T(8,128)(2,1)S(1)}, bf16[4,4,4,32,32]{4,3,2,1,0:T(8,128)(2,1)}, u32[]{:S(2)}) copy-start(bf16[4,4,4,32,32]{4,3,2,1,0:T(8,128)(2,1)} %tr1.3) | copy-start | bytes 393220
  32.3 1.2 %copy-start.4 = (bf16[4,4,32,864]{3,2,1,0:T(8,128)(2,1)S(1)}, bf16[4,4,32,864]{3,2,1,0:T(8,128)(2,1)}, u32[]{:S(2)}) copy-start(bf16[4,4,32,864]{3,2,1,0:T(8,128)(2,1)} %cp1.1) | copy-start | bytes 2654212
  33.5 0.9 copy-start.6
  34.4 0.9 copy-start.8
  35.3 0.9 copy-start.9
  36.2 0.8 copy-start.11
  37.0 0.8 copy-start.13

commit v2 on v1

--- a/solution.py
+++ b/solution.py
@@ -85,15 +85,16 @@
     acc[i, j] += total
 
 
-def near_inside(npk, acc, colb):
-    acc[...] = jnp.zeros(acc.shape, F32)
+def near_inside(npk, acc, colb, part):
 
     def middle(n, _):
         i, j = n // 6, n % 6 + 1
         near_box(npk, acc, colb, i, j, [(0, 1), (1, -1), (1, 0), (1, 1)], [])
         return 0
 
-    lax.fori_loop(0, 42, middle, 0)
+    lax.fori_loop(21 * part, 21 * part + 21, middle, 0)
+    if part == 0:
+        return
 
     def ends(i, _):
         near_box(npk, acc, colb, i, 0, [(0, 1), (1, 0), (1, 1)], [])
@@ -218,7 +219,10 @@
     return dot_t(x.astype(BF), transfer.reshape(128, 32))
 
 
-def send_kernel(off, vec, basis, tr1, tr2, tr3, npk_out, d0_out, e_out, w3_out, npk, d0, e, g1, g2, send, recv, send1, recv1, send2, recv2):
+def kernel(*refs):
+    given, out, (npk, d0, e, g1, g2, acc, colb, send, recv, send1, recv1, send2, recv2, load) = refs[:13], refs[13], refs[27:]
+    held = refs[14:27]
+    off, vec, basis, cp0, cp1, cp2, cp3, cp4, cpt, tr1, tr2, tr3, tr4 = held
     gx, gy = lax.axis_index("gx"), lax.axis_index("gy")
 
     def there(a, b):
@@ -227,6 +231,18 @@
         for test in ([x >= 0] if a < 0 else []) + ([x < NX] if a > 0 else []) + ([y >= 0] if b < 0 else []) + ([y < NY] if b > 0 else []):
             ok = test if ok is None else ok & test
         return ok, x, y
+
+    anc_x, anc_y = gx // 2, gy // 2
+    loads = []
+    for n in range(13):
+        src = given[n].at[anc_x, anc_y] if n == 7 else given[n]
+        loads.append(pltpu.make_async_copy(src, held[n], load.at[n]))
+    first = (0, 1, 2, 9, 10, 11)
+    for n in first:
+        loads[n].start()
+    for n in range(13):
+        if n not in first:
+            loads[n].start()
 
     npk[...] = jnp.zeros(npk.shape, BF)
     d0[...] = jnp.zeros(d0.shape, BF)
@@ -244,6 +260,9 @@
             @pl.when(ok)
             def _():
                 pl.semaphore_signal(barrier, inc=1, device_id=(x, y), device_id_type=MESH)
+
+    for n in first:
+        loads[n].wait()
 
     def pack(i, _):
         for j in range(8):
@@ -323,6 +342,8 @@
             for c in copies:
                 c.start()
 
+    acc[...] = jnp.zeros(acc.shape, F32)
+    near_inside(npk, acc, colb, 0)
     for k in range(1, NY):
         row_copy(k).wait_recv()
     groups = [g1[4 * t] + g1[4 * t + 1] + g1[4 * t + 2] + g1[4 * t + 3] for t in range(4)]
@@ -332,6 +353,8 @@
     for k in range(1, NX):
         col_copy(k).start()
 
+    near_inside(npk, acc, colb, 1)
+
     for a, b in SIDES:
         copies = side_copies(a, b)[1]
 
@@ -340,32 +363,14 @@
             for c in copies:
                 c.wait_recv()
 
-    npk_out[...] = npk[...]
-    d0_out[...] = d0[...]
-    e_out[...] = e[...]
+    near_edges(npk, acc, colb)
+    for n in range(13):
+        if n not in first:
+            loads[n].wait()
     for k in range(1, NX):
         col_copy(k).wait_recv()
-    w3_out[...] = g2[...]
-    for a, b in SIDES:
-        ok, copies = side_copies(a, b)
-
-        @pl.when(ok)
-        def _():
-            for c in copies:
-                c.wait_send()
-
-    for k in range(1, NY):
-        row_copy(k).wait_send()
-    for k in range(1, NX):
-        col_copy(k).wait_send()
-
-
-def rest_kernel(npk, d0, e, w3, basis, cp0, cp1, cp2, cp3, cp4, cpt, tr1, tr2, tr3, tr4, out, acc, colb):
-    gx, gy = lax.axis_index("gx"), lax.axis_index("gy")
-    near_inside(npk, acc, colb)
-    near_edges(npk, acc, colb)
-
-    whole3 = w3[...].astype(F32)
+
+    whole3 = g2[...].astype(F32)
     rows3 = [jnp.concatenate([whole3[i, 0:8], whole3[i, 8:16]], axis=1) for i in range(NX)]
     rows4 = [row_up(rows3[2 * m], rows3[2 * m + 1], tr4, m, NY // 2) for m in range(NX // 2)]
 
@@ -376,13 +381,12 @@
         return got
 
     def read3(r):
-        block = w3[r].astype(F32)
+        block = g2[r].astype(F32)
         return jnp.concatenate([block[0:8], block[8:16]], axis=1)
 
-    anc_x, anc_y = gx // 2, gy // 2
     far3 = far_single(single_window(read3, NX, 32 * NY, gx, gy), cp3[0, 0], gx % 2, gy % 2)
     window4 = single_window(lambda r: select(rows4, r), NX // 2, 16 * NY, anc_x, anc_y)
-    down4 = far_single(window4, cp4[anc_x, anc_y], anc_x % 2, anc_y % 2)
+    down4 = far_single(window4, cp4[...], anc_x % 2, anc_y % 2)
     base_x, base_y = 2 * (anc_x // 2), 2 * (anc_y // 2)
     box_y = lane((8, 16 * NY)) // 32
     near_y = (box_y >= base_y - 2) & (box_y <= base_y + 3)
@@ -439,41 +443,51 @@
                 i, j = 2 * m + t // 2, 2 * n + t % 2
                 out[i, j] = acc[i, j] * (0.0625 * ROOT3) + given[8 * t : 8 * t + 8]
 
-
-def on_device(off, vec, basis, cp0, cp1, cp2, cp3, cp4, cpt, tr1, tr2, tr3, tr4):
-    vmem = pl.BlockSpec(memory_space=pltpu.VMEM)
+    for a, b in SIDES:
+        ok, copies = side_copies(a, b)
+
+        @pl.when(ok)
+        def _():
+            for c in copies:
+                c.wait_send()
+
+    for k in range(1, NY):
+        row_copy(k).wait_send()
+    for k in range(1, NX):
+        col_copy(k).wait_send()
+
+
+HELD = [(8, 8, 2, 256), (8, 8, 8, 256), (8, 8, 32, 256), (8, 8, 32, 864), (4, 4, 32, 864), (2, 2, 32, 864), (1, 1, 32, 864), (32, 864),
+        (1, 1, 32, 2048), (4, 4, 4, 32, 32), (2, 2, 4, 32, 32), (1, 1, 4, 32, 32), (8, 8, 4, 32, 32)]
+
+
+def on_device(*args):
     sem = pltpu.SemaphoreType.DMA
-    shapes = [(10, 10, 16, 256), (6, 16, 512), (7, 16, 384), (NX, 16, 256)]
-    npk, d0, e, w3 = pl.pallas_call(
-        send_kernel,
-        out_shape=[jax.ShapeDtypeStruct(s, BF) for s in shapes],
-        in_specs=[vmem] * 6,
-        out_specs=[vmem] * 4,
-        scratch_shapes=[
-            pltpu.VMEM(shapes[0], BF),
-            pltpu.VMEM(shapes[1], BF),
-            pltpu.VMEM(shapes[2], BF),
+    return pl.pallas_call(
+        kernel,
+        out_shape=jax.ShapeDtypeStruct((8, 8, 8, 256), F32),
+        in_specs=[pl.BlockSpec(memory_space=pl.ANY)] * 13,
+        out_specs=pl.BlockSpec(memory_space=pltpu.VMEM),
+        scratch_shapes=[pltpu.VMEM(s, BF) for s in HELD]
+        + [
+            pltpu.VMEM((10, 10, 16, 256), BF),
+            pltpu.VMEM((6, 16, 512), BF),
+            pltpu.VMEM((7, 16, 384), BF),
             pltpu.VMEM((NY, 8, 128), F32),
-            pltpu.VMEM(shapes[3], BF),
+            pltpu.VMEM((NX, 16, 256), BF),
+            pltpu.VMEM((8, 8, 8, 256), F32),
+            pltpu.VMEM((4, 256, 128), BF),
             sem((8, 3)),
             sem((8, 3)),
             sem((NY,)),
             sem((NY,)),
             sem((NX,)),
             sem((NX,)),
+            sem((13,)),
         ],
-        compiler_params=pltpu.CompilerParams(collective_id=0, has_side_effects=True, vmem_limit_bytes=24 << 20),
-        name="coefficients",
-    )(off, vec, basis, tr1, tr2, tr3)
-    return pl.pallas_call(
-        rest_kernel,
-        out_shape=jax.ShapeDtypeStruct((8, 8, 8, 256), F32),
-        in_specs=[vmem] * 15,
-        out_specs=vmem,
-        scratch_shapes=[pltpu.VMEM((8, 8, 8, 256), F32), pltpu.VMEM((4, 256, 128), BF)],
-        compiler_params=pltpu.CompilerParams(vmem_limit_bytes=48 << 20),
-        name="fields",
-    )(npk, d0, e, w3, basis, cp0, cp1, cp2, cp3, cp4, cpt, tr1, tr2, tr3, tr4)
+        compiler_params=pltpu.CompilerParams(collective_id=0, has_side_effects=True, vmem_limit_bytes=56 << 20),
+        name="product",
+    )(*args)
 
 
 def solution(mesh):

time: 96.9 us -> 69 us (0.71)
  Pallas kernels: 82.8 us -> 67 us
  local copies, waits for them, and re-layouts: 13.5 us -> 1.87 us
    pallas_call x2 -> x1, Pallas kernels: 82.8 us -> 67 us  [on_device(): pl.pallas_call(kernel, out_shape=jax.ShapeDtypeStruct((8, 8, 8, 256), F32...]
    unnamed x28 -> x1, local copies, waits for them, and re-layouts: 13.5 us -> 1.87 us
where the time goes in v2:
time: 69 us; the launch traced here: 68.9 us
  Pallas kernels  67 us (97%)
  local copies, waits for them, and re-layouts  1.87 us (3%)
    pallas_call x1, Pallas kernels, on_device(): pl.pallas_call(kernel, out_shape=jax.ShapeDtypeStruct((8, 8, 8, 256), F32...  67 us
    unnamed x1, local copies, waits for them, and re-layouts  1.87 us

profile of v2, /device:TPU:1, one launch (start us, length us, event | category | flops | bytes accessed | tf_op | source)
XLA Modules:
  0.0 68.9 jit_solution(17976046614140783667)
XLA Ops:
  0.0 67.0 %product.1 = f32[8,8,8,256]{3,2,1,0:T(8,128)} custom-call(bf16[8,8,2,256]{3,2,1,0:T(2,128)(2,1)} %refs_0_.1, bf16[8,8,8,256]{3,2,1,0:T(8,128)(2,1)} %refs_1_.1, bf16[8,8,32,256]{3,2,1,0:T(8,128)(2,1)} %refs_2_.1, bf16[8,8,32,864]{3,2,1,0:T(8,128)(2,1)} %refs_3_.1, bf16[4,4,32,864]{3,2,1,0:T(8,128)(2,1)} %refs_4_.1, bf16[2,2,32,864]{3,2,1,0:T(8,128)(2,1)} %refs_5_.1, ...), custom_call_target="tpu_custom_call" | custom-call | tf_op jit(solution)/shard_map/product/pallas_call | solution.py:466
  67.0 1.9 %copy.15 = f32[8,8,8,256]{3,2,1,0:T(8,128)} copy(f32[8,8,8,256]{3,2,1,0:T(8,128)} %product.1) | data formatting | bytes 1048576

commit v3 on v2

--- a/solution.py
+++ b/solution.py
@@ -41,22 +41,27 @@
     return out
 
 
-def set_columns(npk, colb, hi, hj):
-    rows = npk[hi, hj].astype(F32)[8:16]
-    cols = rows.T
-    for c in range(4):
-        colb[c] = jnp.broadcast_to(cols[:, c : c + 1], (256, 128)).astype(BF)
-
-
-def kernel_tile(npk, colb, yi, yj, step_x, step_y):
+BACK = [(0, 1), (0, -1), (1, 0), (1, 1), (1, -1)]
+AHEAD = [(0, 1), (1, -1), (1, 0), (1, 1)]
+
+
+def set_columns(npk, cols, i, j):
+    rows = npk[i, j + 1].astype(F32)
+    for c in (0, 2):
+        wide = jnp.broadcast_to(rows[8 + c : 9 + c], (128, 256)).T.astype(BF)
+        cols[c] = wide
+        cols[c + 1] = wide - jnp.asarray(1.0, BF)
+
+
+def kernel_tile(npk, cols, yi, yj, step_x, step_y):
     row_x = npk[yi, yj, 9:10] if step_x == -1 else npk[yi, yj, 8:9]
     row_y = npk[yi, yj, 11:12] if step_y == -1 else npk[yi, yj, 10:11]
     col_x = 1 if step_x == 1 else 0
     col_y = 3 if step_y == 1 else 2
     halves = []
     for h in range(2):
-        dx = row_x[:, 128 * h : 128 * h + 128] - colb[col_x]
-        dy = row_y[:, 128 * h : 128 * h + 128] - colb[col_y]
+        dx = row_x[:, 128 * h : 128 * h + 128] - cols[col_x]
+        dy = row_y[:, 128 * h : 128 * h + 128] - cols[col_y]
         r2 = jnp.maximum(dx * dx + dy * dy, jnp.asarray(1e-30, BF))
         r = r2 * lax.rsqrt(r2)
         e = jnp.exp2(r * jnp.asarray(-ROOT3 * LOG2E, BF))
@@ -64,71 +69,39 @@
     return jnp.concatenate(halves, axis=1)
 
 
-def near_box(npk, acc, colb, i, j, forward, one_way, own=True):
-    set_columns(npk, colb, i + 1, j + 1)
-    mine = npk[i + 1, j + 1][0:8] if False else npk[i + 1, j + 1].astype(F32)[0:8].astype(BF)
-    total = None
-    if own:
-        tile = kernel_tile(npk, colb, i + 1, j + 1, 0, 0)
-        total = dot_t(mine, tile)
-    for a, b in forward:
-        tile = kernel_tile(npk, colb, i + 1 + a, j + 1 + b, a, b)
-        other = npk[i + 1 + a, j + 1 + b].astype(F32)[0:8].astype(BF)
-        part = dot_t(other, tile)
-        total = part if total is None else total + part
-        acc[i + a, j + b] += dot_n(mine, tile)
-    for a, b in one_way:
-        tile = kernel_tile(npk, colb, i + 1 + a, j + 1 + b, a, b)
-        other = npk[i + 1 + a, j + 1 + b].astype(F32)[0:8].astype(BF)
-        part = dot_t(other, tile)
-        total = part if total is None else total + part
-    acc[i, j] += total
-
-
-def near_inside(npk, acc, colb, part):
-
-    def middle(n, _):
-        i, j = n // 6, n % 6 + 1
-        near_box(npk, acc, colb, i, j, [(0, 1), (1, -1), (1, 0), (1, 1)], [])
+def near_box(npk, acc, cols, i, j):
+    mine = npk[i, j + 1]
+    total = dot_t(mine, kernel_tile(npk, cols, i, j + 1, 0, 0))
+    for a, b in AHEAD:
+        tile = kernel_tile(npk, cols, i + a, j + 1 + b, a, b)
+        total = total + dot_t(npk[i + a, j + 1 + b], tile)
+        acc[i + a, j + 1 + b] += dot_n(mine, tile)[0:8]
+    acc[i, j + 1] += total[0:8]
+
+
+def near_pairs(npk, acc, cols_a, cols_b, low, high, first, second):
+    set_columns(npk, cols_a, *first(low))
+
+    def body(n, _):
+        set_columns(npk, cols_b, *second(n))
+        near_box(npk, acc, cols_a, *first(n))
+        set_columns(npk, cols_a, *first(jnp.minimum(n + 1, high - 1)))
+        near_box(npk, acc, cols_b, *second(n))
         return 0
 
-    lax.fori_loop(21 * part, 21 * part + 21, middle, 0)
-    if part == 0:
-        return
-
-    def ends(i, _):
-        near_box(npk, acc, colb, i, 0, [(0, 1), (1, 0), (1, 1)], [])
-        near_box(npk, acc, colb, i, 7, [(1, -1), (1, 0)], [])
-        return 0
-
-    lax.fori_loop(0, 7, ends, 0)
-
-    def bottom(j, _):
-        near_box(npk, acc, colb, 7, j, [(0, 1)], [])
-        return 0
-
-    lax.fori_loop(0, 7, bottom, 0)
-    near_box(npk, acc, colb, 7, 7, [], [])
-
-
-def near_edges(npk, acc, colb):
-    def rows(j, _):
-        near_box(npk, acc, colb, 0, j, [], [(-1, -1), (-1, 0), (-1, 1)], own=False)
-        near_box(npk, acc, colb, 7, j, [], [(1, -1), (1, 0), (1, 1)], own=False)
-        return 0
-
-    lax.fori_loop(0, 8, rows, 0)
-
-    def cols(i, _):
-        near_box(npk, acc, colb, i, 0, [], [(-1, -1), (0, -1), (1, -1)], own=False)
-        near_box(npk, acc, colb, i, 7, [], [(-1, 1), (0, 1), (1, 1)], own=False)
-        return 0
-
-    lax.fori_loop(1, 7, cols, 0)
-    near_box(npk, acc, colb, 0, 0, [], [(0, -1), (1, -1)], own=False)
-    near_box(npk, acc, colb, 7, 0, [], [(-1, -1), (0, -1)], own=False)
-    near_box(npk, acc, colb, 0, 7, [], [(0, 1), (1, 1)], own=False)
-    near_box(npk, acc, colb, 7, 7, [], [(-1, 1), (0, 1)], own=False)
+    lax.fori_loop(low, high, body, 0)
+
+
+def near_middle(npk, acc, cols_a, cols_b, low, high):
+    near_pairs(
+        npk, acc, cols_a, cols_b, low, high,
+        lambda n: (n // 3, 2 * (n % 3) + 1), lambda n: (n // 3, 2 * (n % 3) + 2),
+    )
+
+
+def near_border(npk, acc, cols_a, cols_b):
+    near_pairs(npk, acc, cols_a, cols_b, 0, 7, lambda n: (n, 0), lambda n: (n, 7))
+    near_pairs(npk, acc, cols_a, cols_b, 0, 4, lambda n: (7, 2 * n), lambda n: (7, 2 * n + 1))
 
 
 def own_coefficients(vec, basis, i):
@@ -220,7 +193,7 @@
 
 
 def kernel(*refs):
-    given, out, (npk, d0, e, g1, g2, acc, colb, send, recv, send1, recv1, send2, recv2, load) = refs[:13], refs[13], refs[27:]
+    given, out, (npk, d0, e, g1, g2, acc, cols_a, cols_b, back_s, back_r, back_c, send, recv, send1, recv1, send2, recv2, send3, recv3, load) = refs[:13], refs[13], refs[27:]
     held = refs[14:27]
     off, vec, basis, cp0, cp1, cp2, cp3, cp4, cpt, tr1, tr2, tr3, tr4 = held
     gx, gy = lax.axis_index("gx"), lax.axis_index("gy")
@@ -247,6 +220,9 @@
     npk[...] = jnp.zeros(npk.shape, BF)
     d0[...] = jnp.zeros(d0.shape, BF)
     e[...] = jnp.zeros(e.shape, BF)
+    back_s[...] = jnp.zeros(back_s.shape, F32)
+    back_r[...] = jnp.zeros(back_r.shape, F32)
+    back_c[...] = jnp.zeros(back_c.shape, F32)
 
     barrier = pltpu.get_barrier_semaphore()
     for k in range(1, NX):
@@ -269,7 +245,7 @@
             o = off[i, j].astype(F32)
             v = vec[i, j].astype(F32)
             x, y = o[0:1], o[1:2]
-            npk[i + 1, j + 1] = jnp.concatenate([v, x, x - 1.0, y, y - 1.0, jnp.zeros((4, 256), F32)], axis=0).astype(BF)
+            npk[i, j + 1] = jnp.concatenate([v, x, x - 1.0, y, y - 1.0, jnp.zeros((4, 256), F32)], axis=0).astype(BF)
         return 0
 
     lax.fori_loop(0, 8, pack, 0)
@@ -312,15 +288,13 @@
         ok, x, y = there(a, b)
         n = SIDES.index((a, b))
 
-        def part(step, low, high, count):
-            return {0: (low, low, count), 1: (high[0], high[1], high[2]), -1: (low, count + low, high[2])}[step]
-
-        rows = {0: (1, 1, 8), 1: (8, 0, 1), -1: (1, 9, 1)}
+        rows = {0: (0, 0, 8), -1: (0, 8, 1), 1: (0, 0, 8)}
+        columns = {0: (1, 1, 8), 1: (8, 0, 1), -1: (1, 9, 1)}
         r0 = {0: (1, 1, 4), 1: (4, 0, 1), -1: (1, 5, 1)}[a]
         l0 = {0: (128, 128, 256), 1: (256, 0, 128), -1: (128, 384, 128)}[b]
         r1 = {0: (2, 2, 3), 1: (3, 0, 2), -1: (2, 5, 2)}[a]
         l1 = {0: (128, 128, 128), 1: (128, 0, 128), -1: (128, 256, 128)}[b]
-        ra, rb = rows[a], rows[b]
+        ra, rb = rows[a], columns[b]
 
         def remote(src, dst, t):
             return pltpu.make_async_remote_copy(
@@ -328,11 +302,28 @@
                 device_id=(x, y), device_id_type=MESH,
             )
 
-        return ok, [
+        copies = [
             remote(d0.at[pl.ds(r0[0], r0[2]), :, pl.ds(l0[0], l0[2])], d0.at[pl.ds(r0[1], r0[2]), :, pl.ds(l0[1], l0[2])], 0),
             remote(e.at[pl.ds(r1[0], r1[2]), :, pl.ds(l1[0], l1[2])], e.at[pl.ds(r1[1], r1[2]), :, pl.ds(l1[1], l1[2])], 1),
-            remote(npk.at[pl.ds(ra[0], ra[2]), pl.ds(rb[0], rb[2])], npk.at[pl.ds(ra[1], ra[2]), pl.ds(rb[1], rb[2])], 2),
         ]
+        if a < 1 and (a, b) != (0, 0):
+            copies.append(
+                remote(npk.at[pl.ds(ra[0], ra[2]), pl.ds(rb[0], rb[2])], npk.at[pl.ds(ra[1], ra[2]), pl.ds(rb[1], rb[2])], 2)
+            )
+        return ok, copies
+
+    def back_copies(a, b):
+        ok, x, y = there(a, b)
+        n = BACK.index((a, b))
+        rows, column = (8 if a else pl.ds(0, 8)), {0: pl.ds(1, 8), 1: 9, -1: 0}[b]
+        if a and b:
+            dst = back_c.at[n - 3]
+        else:
+            dst = back_r if a else back_s.at[n]
+        return ok, pltpu.make_async_remote_copy(
+            src_ref=acc.at[rows, column], dst_ref=dst, send_sem=send3.at[n], recv_sem=recv3.at[n],
+            device_id=(x, y), device_id_type=MESH,
+        )
 
     for a, b in SIDES:
         ok, copies = side_copies(a, b)
@@ -343,7 +334,7 @@
                 c.start()
 
     acc[...] = jnp.zeros(acc.shape, F32)
-    near_inside(npk, acc, colb, 0)
+    near_middle(npk, acc, cols_a, cols_b, 0, 10)
     for k in range(1, NY):
         row_copy(k).wait_recv()
     groups = [g1[4 * t] + g1[4 * t + 1] + g1[4 * t + 2] + g1[4 * t + 3] for t in range(4)]
@@ -353,7 +344,7 @@
     for k in range(1, NX):
         col_copy(k).start()
 
-    near_inside(npk, acc, colb, 1)
+    near_middle(npk, acc, cols_a, cols_b, 10, 21)
 
     for a, b in SIDES:
         copies = side_copies(a, b)[1]
@@ -363,7 +354,14 @@
             for c in copies:
                 c.wait_recv()
 
-    near_edges(npk, acc, colb)
+    near_border(npk, acc, cols_a, cols_b)
+    for a, b in BACK:
+        ok, back = back_copies(a, b)
+
+        @pl.when(ok)
+        def _():
+            back.start()
+
     for n in range(13):
         if n not in first:
             loads[n].wait()
@@ -428,6 +426,13 @@
         rows += [block[0:8], block[8:16]]
     moved = [shifted(row) for row in rows]
     group = lane((8, 128)) // 32
+    for a, b in BACK:
+        back = back_copies(a, b)[1]
+
+        @pl.when(there(-a, -b)[0])
+        def _():
+            back.wait_recv()
+
     for m in range(4):
         for n in range(4):
             window = []
@@ -441,7 +446,18 @@
             given = dot_n(parts, four(basis, m, n))
             for t in range(4):
                 i, j = 2 * m + t // 2, 2 * n + t % 2
-                out[i, j] = acc[i, j] * (0.0625 * ROOT3) + given[8 * t : 8 * t + 8]
+                near = acc[i, j + 1]
+                if j == 0:
+                    near = near + back_s[0, i]
+                if j == 7:
+                    near = near + back_s[1, i]
+                if i == 0:
+                    near = near + back_r[j]
+                if (i, j) == (0, 0):
+                    near = near + back_c[0]
+                if (i, j) == (0, 7):
+                    near = near + back_c[1]
+                out[i, j] = near * (0.0625 * ROOT3) + given[8 * t : 8 * t + 8]
 
     for a, b in SIDES:
         ok, copies = side_copies(a, b)
@@ -450,6 +466,13 @@
         def _():
             for c in copies:
                 c.wait_send()
+
+    for a, b in BACK:
+        ok, back = back_copies(a, b)
+
+        @pl.when(ok)
+        def _():
+            back.wait_send()
 
     for k in range(1, NY):
         row_copy(k).wait_send()
@@ -470,19 +493,25 @@
         out_specs=pl.BlockSpec(memory_space=pltpu.VMEM),
         scratch_shapes=[pltpu.VMEM(s, BF) for s in HELD]
         + [
-            pltpu.VMEM((10, 10, 16, 256), BF),
+            pltpu.VMEM((9, 10, 16, 256), BF),
             pltpu.VMEM((6, 16, 512), BF),
             pltpu.VMEM((7, 16, 384), BF),
             pltpu.VMEM((NY, 8, 128), F32),
             pltpu.VMEM((NX, 16, 256), BF),
-            pltpu.VMEM((8, 8, 8, 256), F32),
+            pltpu.VMEM((9, 10, 8, 256), F32),
             pltpu.VMEM((4, 256, 128), BF),
+            pltpu.VMEM((4, 256, 128), BF),
+            pltpu.VMEM((2, 8, 8, 256), F32),
+            pltpu.VMEM((8, 8, 256), F32),
+            pltpu.VMEM((2, 8, 256), F32),
             sem((8, 3)),
             sem((8, 3)),
             sem((NY,)),
             sem((NY,)),
             sem((NX,)),
             sem((NX,)),
+            sem((5,)),
+            sem((5,)),
             sem((13,)),
         ],
         compiler_params=pltpu.CompilerParams(collective_id=0, has_side_effects=True, vmem_limit_bytes=56 << 20),

time: 69 us -> 50.7 us (0.73)
  Pallas kernels: 67 us -> 48 us
    pallas_call x1, Pallas kernels: 67 us -> 48 us  [on_device(): pl.pallas_call(kernel, out_shape=jax.ShapeDtypeStruct((8, 8, 8, 256), F32...]
where the time goes in v3:
time: 50.7 us; the launch traced here: 49.9 us
  Pallas kernels  48 us (95%)
  local copies, waits for them, and re-layouts  1.87 us (4%)
    pallas_call x1, Pallas kernels, on_device(): pl.pallas_call(kernel, out_shape=jax.ShapeDtypeStruct((8, 8, 8, 256), F32...  48 us
    unnamed x1, local copies, waits for them, and re-layouts  1.87 us

profile of v3, /device:TPU:1, one launch (start us, length us, event | category | flops | bytes accessed | tf_op | source)
XLA Modules:
  0.0 49.9 jit_solution(15437542280597392787)
XLA Ops:
  0.0 48.0 %product.1 = f32[8,8,8,256]{3,2,1,0:T(8,128)} custom-call(bf16[8,8,2,256]{3,2,1,0:T(2,128)(2,1)} %refs_0_.1, bf16[8,8,8,256]{3,2,1,0:T(8,128)(2,1)} %refs_1_.1, bf16[8,8,32,256]{3,2,1,0:T(8,128)(2,1)} %refs_2_.1, bf16[8,8,32,864]{3,2,1,0:T(8,128)(2,1)} %refs_3_.1, bf16[4,4,32,864]{3,2,1,0:T(8,128)(2,1)} %refs_4_.1, bf16[2,2,32,864]{3,2,1,0:T(8,128)(2,1)} %refs_5_.1, ...), custom_call_target="tpu_custom_call" | custom-call | tf_op jit(solution)/shard_map/product/pallas_call | solution.py:489
  48.0 1.9 %copy.15 = f32[8,8,8,256]{3,2,1,0:T(8,128)} copy(f32[8,8,8,256]{3,2,1,0:T(8,128)} %product.1) | data formatting | bytes 1048576

commit v4 on v3

--- a/solution.py
+++ b/solution.py
@@ -53,25 +53,29 @@
         cols[c + 1] = wide - jnp.asarray(1.0, BF)
 
 
+def kernel_piece(npk, cols, yi, yj, step_x, step_y, half, low, high):
+    lanes = slice(128 * half, 128 * half + 128)
+    row_x = npk[yi, yj, 9:10, lanes] if step_x == -1 else npk[yi, yj, 8:9, lanes]
+    row_y = npk[yi, yj, 11:12, lanes] if step_y == -1 else npk[yi, yj, 10:11, lanes]
+    dx = row_x - cols[1 if step_x == 1 else 0, low:high]
+    dy = row_y - cols[3 if step_y == 1 else 2, low:high]
+    r2 = jnp.maximum(dx * dx + dy * dy, jnp.asarray(1e-30, BF))
+    r = r2 * lax.rsqrt(r2)
+    e = jnp.exp2(r * jnp.asarray(-ROOT3 * LOG2E, BF))
+    return (r + jnp.asarray(1.0 / ROOT3, BF)) * e
+
+
 def kernel_tile(npk, cols, yi, yj, step_x, step_y):
-    row_x = npk[yi, yj, 9:10] if step_x == -1 else npk[yi, yj, 8:9]
-    row_y = npk[yi, yj, 11:12] if step_y == -1 else npk[yi, yj, 10:11]
-    col_x = 1 if step_x == 1 else 0
-    col_y = 3 if step_y == 1 else 2
-    halves = []
-    for h in range(2):
-        dx = row_x[:, 128 * h : 128 * h + 128] - cols[col_x]
-        dy = row_y[:, 128 * h : 128 * h + 128] - cols[col_y]
-        r2 = jnp.maximum(dx * dx + dy * dy, jnp.asarray(1e-30, BF))
-        r = r2 * lax.rsqrt(r2)
-        e = jnp.exp2(r * jnp.asarray(-ROOT3 * LOG2E, BF))
-        halves.append((r + jnp.asarray(1.0 / ROOT3, BF)) * e)
-    return jnp.concatenate(halves, axis=1)
+    return jnp.concatenate([kernel_piece(npk, cols, yi, yj, step_x, step_y, h, 0, 256) for h in range(2)], axis=1)
 
 
 def near_box(npk, acc, cols, i, j):
     mine = npk[i, j + 1]
-    total = dot_t(mine, kernel_tile(npk, cols, i, j + 1, 0, 0))
+    left = kernel_piece(npk, cols, i, j + 1, 0, 0, 0, 0, 128)
+    cross = kernel_piece(npk, cols, i, j + 1, 0, 0, 1, 0, 128)
+    right = kernel_piece(npk, cols, i, j + 1, 0, 0, 1, 128, 256)
+    v0, v1 = mine[:, 0:128], mine[:, 128:256]
+    total = jnp.concatenate([dot_n(v0, left) + dot_t(v1, cross), dot_n(v0, cross) + dot_n(v1, right)], axis=1)
     for a, b in AHEAD:
         tile = kernel_tile(npk, cols, i + a, j + 1 + b, a, b)
         total = total + dot_t(npk[i + a, j + 1 + b], tile)
@@ -79,29 +83,31 @@
     acc[i, j + 1] += total[0:8]
 
 
-def near_pairs(npk, acc, cols_a, cols_b, low, high, first, second):
-    set_columns(npk, cols_a, *first(low))
+def near_order(n):
+    m, k = jnp.maximum(n - 21, 0), jnp.maximum(n - 28, 0)
+    inside, sides = n < 21, n < 28
+
+    def pick(a, b, c):
+        return jnp.where(inside, a, jnp.where(sides, b, c))
+
+    row = pick(n // 3, m, 7)
+    return (row, pick(2 * (n % 3) + 1, 0, 2 * k)), (row, pick(2 * (n % 3) + 2, 7, 2 * k + 1))
+
+
+def near_field(npk, acc, cols_a, cols_b, events):
+    set_columns(npk, cols_a, *near_order(jnp.int32(0))[0])
 
     def body(n, _):
-        set_columns(npk, cols_b, *second(n))
-        near_box(npk, acc, cols_a, *first(n))
-        set_columns(npk, cols_a, *first(jnp.minimum(n + 1, high - 1)))
-        near_box(npk, acc, cols_b, *second(n))
+        for step, event in events:
+            pl.when(n == step)(event)
+        first, second = near_order(n)
+        set_columns(npk, cols_b, *second)
+        near_box(npk, acc, cols_a, *first)
+        set_columns(npk, cols_a, *near_order(jnp.minimum(n + 1, 31))[0])
+        near_box(npk, acc, cols_b, *second)
         return 0
 
-    lax.fori_loop(low, high, body, 0)
-
-
-def near_middle(npk, acc, cols_a, cols_b, low, high):
-    near_pairs(
-        npk, acc, cols_a, cols_b, low, high,
-        lambda n: (n // 3, 2 * (n % 3) + 1), lambda n: (n // 3, 2 * (n % 3) + 2),
-    )
-
-
-def near_border(npk, acc, cols_a, cols_b):
-    near_pairs(npk, acc, cols_a, cols_b, 0, 7, lambda n: (n, 0), lambda n: (n, 7))
-    near_pairs(npk, acc, cols_a, cols_b, 0, 4, lambda n: (7, 2 * n), lambda n: (7, 2 * n + 1))
+    lax.fori_loop(0, 32, body, 0)
 
 
 def own_coefficients(vec, basis, i):
@@ -193,7 +199,7 @@
 
 
 def kernel(*refs):
-    given, out, (npk, d0, e, g1, g2, acc, cols_a, cols_b, back_s, back_r, back_c, send, recv, send1, recv1, send2, recv2, send3, recv3, load) = refs[:13], refs[13], refs[27:]
+    given, out, (npk, f, ga, gb, g2, acc, cols_a, cols_b, back_s, back_r, back_c, result, send, recv, sends, recvs, send3, recv3, load, store) = refs[:13], refs[13], refs[27:]
     held = refs[14:27]
     off, vec, basis, cp0, cp1, cp2, cp3, cp4, cpt, tr1, tr2, tr3, tr4 = held
     gx, gy = lax.axis_index("gx"), lax.axis_index("gy")
@@ -218,24 +224,41 @@
             loads[n].start()
 
     npk[...] = jnp.zeros(npk.shape, BF)
-    d0[...] = jnp.zeros(d0.shape, BF)
-    e[...] = jnp.zeros(e.shape, BF)
+    f[...] = jnp.zeros(f.shape, BF)
     back_s[...] = jnp.zeros(back_s.shape, F32)
     back_r[...] = jnp.zeros(back_r.shape, F32)
     back_c[...] = jnp.zeros(back_c.shape, F32)
 
     barrier = pltpu.get_barrier_semaphore()
-    for k in range(1, NX):
-        pl.semaphore_signal(barrier, inc=1, device_id=(lax.rem(gx + k, NX), gy), device_id_type=MESH)
-    for k in range(1, NY):
-        pl.semaphore_signal(barrier, inc=1, device_id=(gx, lax.rem(gy + k, NY)), device_id_type=MESH)
+
+    def partner(stage, k):
+        if stage == 0:
+            return gx, 4 * (gy // 4) + (gy + k) % 4
+        if stage == 1:
+            return gx, (gy + 4 * k) % NY
+        if stage == 2:
+            return 4 * (gx // 4) + (gx + k) % 4, gy
+        return (gx + 4 * k) % NX, gy
+
+    def greeted(a, b):
+        ok, x, y = there(a, b)
+        if not a:
+            ok = ok & (gy % 4 == (3 if b > 0 else 0))
+        if not b:
+            ok = ok & (gx % 4 == (3 if a > 0 else 0))
+        return ok, x, y
+
+    for stage in range(4):
+        for k in range(1, 4):
+            pl.semaphore_signal(barrier, inc=1, device_id=partner(stage, k), device_id_type=MESH)
+    peers = jnp.int32(12)
     for a, b in SIDES:
-        if a and b:
-            ok, x, y = there(a, b)
-
-            @pl.when(ok)
-            def _():
-                pl.semaphore_signal(barrier, inc=1, device_id=(x, y), device_id_type=MESH)
+        ok, x, y = greeted(a, b)
+        peers = peers + ok.astype(jnp.int32)
+
+        @pl.when(ok)
+        def _():
+            pl.semaphore_signal(barrier, inc=1, device_id=(x, y), device_id_type=MESH)
 
     for n in first:
         loads[n].wait()
@@ -251,38 +274,47 @@
     lax.fori_loop(0, 8, pack, 0)
 
     c0 = [own_coefficients(vec, basis, i) for i in range(8)]
-    for m in range(4):
-        d0[1 + m, :, 128:384] = jnp.concatenate([c0[2 * m], c0[2 * m + 1]], axis=0).astype(BF)
+    for m, at in enumerate((4, 3, 9, 8)):
+        f[at, :, 128:384] = jnp.concatenate([c0[2 * m], c0[2 * m + 1]], axis=0).astype(BF)
     c1 = [row_up(c0[2 * m], c0[2 * m + 1], tr1, m, 4) for m in range(4)]
-    e[2, :, 128:256] = jnp.concatenate([c1[0], c1[1]], axis=0).astype(BF)
-    e[4, :, 128:256] = jnp.concatenate([c1[2], c1[3]], axis=0).astype(BF)
     blank = jnp.zeros((8, 64), F32)
     c2 = [jnp.concatenate([row_up(c1[2 * m], c1[2 * m + 1], tr2, m, 2), blank], axis=1) for m in range(2)]
-    e[3, :, 128:256] = jnp.concatenate([c2[0], c2[1]], axis=0).astype(BF)
+    for at, upper, lower in ((5, c1[0], c1[1]), (6, c2[0], c2[1]), (7, c1[2], c1[3])):
+        block = jnp.concatenate([upper, lower], axis=0).astype(BF)
+        f[at, :, 128:256] = block
+        f[at, :, 256:384] = block
     c3 = row_up(c2[0], c2[1], tr3, 0, 1)
     mine = jnp.concatenate([c3] * 4, axis=1)
-    g1[gy] = jnp.where(lane((8, 128)) // 32 == lax.rem(gy, 4), mine, 0.0)
-
-    beside_x = (gx > 0).astype(jnp.int32) + (gx < NX - 1).astype(jnp.int32)
-    beside_y = (gy > 0).astype(jnp.int32) + (gy < NY - 1).astype(jnp.int32)
-    pl.semaphore_wait(barrier, NX - 1 + NY - 1 + beside_x * beside_y)
-
-    def row_copy(k):
-        other = lax.rem(gy + k, NY)
-        return pltpu.make_async_remote_copy(
-            src_ref=g1.at[gy], dst_ref=g1.at[gy], send_sem=send1.at[k], recv_sem=recv1.at[NY - k],
-            device_id=(gx, other), device_id_type=MESH,
-        )
-
-    def col_copy(k):
-        other = lax.rem(gx + k, NX)
-        return pltpu.make_async_remote_copy(
-            src_ref=g2.at[gx], dst_ref=g2.at[gx], send_sem=send2.at[k], recv_sem=recv2.at[NX - k],
-            device_id=(other, gy), device_id_type=MESH,
-        )
-
-    for k in range(1, NY):
-        row_copy(k).start()
+    ga[gy % 4] = jnp.where(lane((8, 128)) // 32 == gy % 4, mine, 0.0)
+
+    pl.semaphore_wait(barrier, peers)
+
+    def stage_copies(stage):
+        if stage == 0:
+            ref = ga.at[gy % 4]
+        elif stage == 1:
+            ref = gb.at[gy // 4]
+        elif stage == 2:
+            ref = g2.at[gx]
+        else:
+            ref = g2.at[pl.ds(4 * (gx // 4), 4)]
+        return [
+            pltpu.make_async_remote_copy(
+                src_ref=ref, dst_ref=ref, send_sem=sends.at[stage, k], recv_sem=recvs.at[stage, 4 - k],
+                device_id=partner(stage, k), device_id_type=MESH,
+            )
+            for k in range(1, 4)
+        ]
+
+    def start_stage(stage):
+        for c in stage_copies(stage):
+            c.start()
+
+    def end_stage(stage):
+        for c in stage_copies(stage):
+            c.wait_recv()
+
+    start_stage(0)
 
     def side_copies(a, b):
         ok, x, y = there(a, b)
@@ -290,10 +322,8 @@
 
         rows = {0: (0, 0, 8), -1: (0, 8, 1), 1: (0, 0, 8)}
         columns = {0: (1, 1, 8), 1: (8, 0, 1), -1: (1, 9, 1)}
-        r0 = {0: (1, 1, 4), 1: (4, 0, 1), -1: (1, 5, 1)}[a]
+        r0 = {0: (3, 3, 7), 1: (6, 0, 3), -1: (4, 10, 3)}[a]
         l0 = {0: (128, 128, 256), 1: (256, 0, 128), -1: (128, 384, 128)}[b]
-        r1 = {0: (2, 2, 3), 1: (3, 0, 2), -1: (2, 5, 2)}[a]
-        l1 = {0: (128, 128, 128), 1: (128, 0, 128), -1: (128, 256, 128)}[b]
         ra, rb = rows[a], columns[b]
 
         def remote(src, dst, t):
@@ -303,12 +333,11 @@
             )
 
         copies = [
-            remote(d0.at[pl.ds(r0[0], r0[2]), :, pl.ds(l0[0], l0[2])], d0.at[pl.ds(r0[1], r0[2]), :, pl.ds(l0[1], l0[2])], 0),
-            remote(e.at[pl.ds(r1[0], r1[2]), :, pl.ds(l1[0], l1[2])], e.at[pl.ds(r1[1], r1[2]), :, pl.ds(l1[1], l1[2])], 1),
+            remote(f.at[pl.ds(r0[0], r0[2]), :, pl.ds(l0[0], l0[2])], f.at[pl.ds(r0[1], r0[2]), :, pl.ds(l0[1], l0[2])], 0),
         ]
         if a < 1 and (a, b) != (0, 0):
             copies.append(
-                remote(npk.at[pl.ds(ra[0], ra[2]), pl.ds(rb[0], rb[2])], npk.at[pl.ds(ra[1], ra[2]), pl.ds(rb[1], rb[2])], 2)
+                remote(npk.at[pl.ds(ra[0], ra[2]), pl.ds(rb[0], rb[2])], npk.at[pl.ds(ra[1], ra[2]), pl.ds(rb[1], rb[2])], 1)
             )
         return ok, copies
 
@@ -334,27 +363,33 @@
                 c.start()
 
     acc[...] = jnp.zeros(acc.shape, F32)
-    near_middle(npk, acc, cols_a, cols_b, 0, 10)
-    for k in range(1, NY):
-        row_copy(k).wait_recv()
-    groups = [g1[4 * t] + g1[4 * t + 1] + g1[4 * t + 2] + g1[4 * t + 3] for t in range(4)]
-    g2[gx] = jnp.concatenate(
-        [jnp.concatenate(groups[0:2], axis=1), jnp.concatenate(groups[2:4], axis=1)], axis=0
-    ).astype(BF)
-    for k in range(1, NX):
-        col_copy(k).start()
-
-    near_middle(npk, acc, cols_a, cols_b, 10, 21)
-
-    for a, b in SIDES:
-        copies = side_copies(a, b)[1]
-
-        @pl.when(there(-a, -b)[0])
-        def _():
-            for c in copies:
-                c.wait_recv()
-
-    near_border(npk, acc, cols_a, cols_b)
+
+    def after_a():
+        end_stage(0)
+        gb[gy // 4] = ga[0] + ga[1] + ga[2] + ga[3]
+        start_stage(1)
+
+    def after_b():
+        end_stage(1)
+        upper = jnp.concatenate([gb[0], gb[1]], axis=1)
+        lower = jnp.concatenate([gb[2], gb[3]], axis=1)
+        g2[gx] = jnp.concatenate([upper, lower], axis=0).astype(BF)
+        start_stage(2)
+
+    def after_c():
+        end_stage(2)
+        start_stage(3)
+
+    def arrived():
+        for a, b in SIDES:
+            copies = side_copies(a, b)[1]
+
+            @pl.when(there(-a, -b)[0])
+            def _():
+                for c in copies:
+                    c.wait_recv()
+
+    near_field(npk, acc, cols_a, cols_b, [(5, after_a), (10, after_b), (15, after_c), (21, arrived)])
     for a, b in BACK:
         ok, back = back_copies(a, b)
 
@@ -365,8 +400,7 @@
     for n in range(13):
         if n not in first:
             loads[n].wait()
-    for k in range(1, NX):
-        col_copy(k).wait_recv()
+    end_stage(3)
 
     whole3 = g2[...].astype(F32)
     rows3 = [jnp.concatenate([whole3[i, 0:8], whole3[i, 8:16]], axis=1) for i in range(NX)]
@@ -397,17 +431,17 @@
     own4 = dot_t(down4.astype(BF), tr4[anc_x, anc_y, slot])
     down3 = far3 + top + own4
 
-    tiles = [e[t].astype(F32) for t in (1 - 1, 3, 6)]
-    tiles = [e[0].astype(F32), e[3].astype(F32), e[6].astype(F32)]
+    tiles = [f[0].astype(F32), f[6].astype(F32), f[12].astype(F32)]
     window = []
     for t in tiles:
-        wide = jnp.concatenate([t[:, 0:64], t[:, 128:192], t[:, 256:320]], axis=1)
+        wide = jnp.concatenate([t[:, 0:64], t[:, 128:192], t[:, 384:448]], axis=1)
         window += [wide[0:8], wide[8:16]]
     down2 = far_parent(window, four(cp2, 0, 0)) + spread(down3, tr3[0, 0])
 
     rows = []
-    for t in (1, 2, 4, 5):
-        block = e[t].astype(F32)
+    for t in (1, 5, 7, 11):
+        block = f[t].astype(F32)
+        block = jnp.concatenate([block[:, 0:256], block[:, 384:512]], axis=1)
         rows += [block[0:8], block[8:16]]
     moved = [shifted(row) for row in rows]
     down1 = {}
@@ -421,8 +455,8 @@
             down1[m, n] = far + spread(slot_part(down2, 2 * m + n), tr2[m, n])
 
     rows = []
-    for t in range(6):
-        block = d0[t].astype(F32)
+    for t in (2, 4, 3, 9, 8, 10):
+        block = f[t].astype(F32)
         rows += [block[0:8], block[8:16]]
     moved = [shifted(row) for row in rows]
     group = lane((8, 128)) // 32
@@ -433,6 +467,7 @@
         def _():
             back.wait_recv()
 
+    stores = []
     for m in range(4):
         for n in range(4):
             window = []
@@ -457,7 +492,9 @@
                     near = near + back_c[0]
                 if (i, j) == (0, 7):
                     near = near + back_c[1]
-                out[i, j] = near * (0.0625 * ROOT3) + given[8 * t : 8 * t + 8]
+                result[i, j] = near * (0.0625 * ROOT3) + given[8 * t : 8 * t + 8]
+        stores.append(pltpu.make_async_copy(result.at[pl.ds(2 * m, 2)], out.at[pl.ds(2 * m, 2)], store.at[m]))
+        stores[m].start()
 
     for a, b in SIDES:
         ok, copies = side_copies(a, b)
@@ -474,10 +511,11 @@
         def _():
             back.wait_send()
 
-    for k in range(1, NY):
-        row_copy(k).wait_send()
-    for k in range(1, NX):
-        col_copy(k).wait_send()
+    for stage in range(4):
+        for c in stage_copies(stage):
+            c.wait_send()
+    for c in stores:
+        c.wait()
 
 
 HELD = [(8, 8, 2, 256), (8, 8, 8, 256), (8, 8, 32, 256), (8, 8, 32, 864), (4, 4, 32, 864), (2, 2, 32, 864), (1, 1, 32, 864), (32, 864),
@@ -490,13 +528,13 @@
         kernel,
         out_shape=jax.ShapeDtypeStruct((8, 8, 8, 256), F32),
         in_specs=[pl.BlockSpec(memory_space=pl.ANY)] * 13,
-        out_specs=pl.BlockSpec(memory_space=pltpu.VMEM),
+        out_specs=pl.BlockSpec(memory_space=pl.ANY),
         scratch_shapes=[pltpu.VMEM(s, BF) for s in HELD]
         + [
             pltpu.VMEM((9, 10, 16, 256), BF),
-            pltpu.VMEM((6, 16, 512), BF),
-            pltpu.VMEM((7, 16, 384), BF),
-            pltpu.VMEM((NY, 8, 128), F32),
+            pltpu.VMEM((13, 16, 512), BF),
+            pltpu.VMEM((4, 8, 128), F32),
+            pltpu.VMEM((4, 8, 128), F32),
             pltpu.VMEM((NX, 16, 256), BF),
             pltpu.VMEM((9, 10, 8, 256), F32),
             pltpu.VMEM((4, 256, 128), BF),
@@ -504,15 +542,15 @@
             pltpu.VMEM((2, 8, 8, 256), F32),
             pltpu.VMEM((8, 8, 256), F32),
             pltpu.VMEM((2, 8, 256), F32),
-            sem((8, 3)),
-            sem((8, 3)),
-            sem((NY,)),
-            sem((NY,)),
-            sem((NX,)),
-            sem((NX,)),
+            pltpu.VMEM((8, 8, 8, 256), F32),
+            sem((8, 2)),
+            sem((8, 2)),
+            sem((4, 4)),
+            sem((4, 4)),
             sem((5,)),
             sem((5,)),
             sem((13,)),
+            sem((4,)),
         ],
         compiler_params=pltpu.CompilerParams(collective_id=0, has_side_effects=True, vmem_limit_bytes=56 << 20),
         name="product",

time: 50.7 us -> 48.5 us (0.957); the launches traced: 49.9 us -> 48.4 us
  Pallas kernels: 48 us -> 46.5 us
    pallas_call x1, Pallas kernels: 48 us -> 46.5 us  [on_device(): pl.pallas_call(kernel, out_shape=jax.ShapeDtypeStruct((8, 8, 8, 256), F32...]
where the time goes in v4:
time: 48.5 us; the launch traced here: 48.4 us
  Pallas kernels  46.5 us (96%)
  local copies, waits for them, and re-layouts  1.87 us (4%)
    pallas_call x1, Pallas kernels, on_device(): pl.pallas_call(kernel, out_shape=jax.ShapeDtypeStruct((8, 8, 8, 256), F32...  46.5 us
    unnamed x1, local copies, waits for them, and re-layouts  1.87 us

profile of v4, /device:TPU:1, one launch (start us, length us, event | category | flops | bytes accessed | tf_op | source)
XLA Modules:
  0.0 48.4 jit_solution(14493957219713075432)
XLA Ops:
  0.0 46.5 %product.1 = f32[8,8,8,256]{3,2,1,0:T(8,128)} custom-call(bf16[8,8,2,256]{3,2,1,0:T(2,128)(2,1)} %refs_0_.1, bf16[8,8,8,256]{3,2,1,0:T(8,128)(2,1)} %refs_1_.1, bf16[8,8,32,256]{3,2,1,0:T(8,128)(2,1)} %refs_2_.1, bf16[8,8,32,864]{3,2,1,0:T(8,128)(2,1)} %refs_3_.1, bf16[4,4,32,864]{3,2,1,0:T(8,128)(2,1)} %refs_4_.1, bf16[2,2,32,864]{3,2,1,0:T(8,128)(2,1)} %refs_5_.1, ...), custom_call_target="tpu_custom_call" | custom-call | tf_op jit(solution)/shard_map/product/pallas_call | solution.py:527
  46.5 1.9 %copy.15 = f32[8,8,8,256]{3,2,1,0:T(8,128)} copy(f32[8,8,8,256]{3,2,1,0:T(8,128)} %product.1) | data formatting | bytes 1048576

commit v5 on v4

--- a/solution.py
+++ b/solution.py
@@ -84,30 +84,35 @@
 
 
 def near_order(n):
-    m, k = jnp.maximum(n - 21, 0), jnp.maximum(n - 28, 0)
-    inside, sides = n < 21, n < 28
+    middle, side, last = n - 11 * (n // 21), n - 10, n - 17
+    border, sides = (n // 10 >= 1) & (n // 21 == 0), n // 17 == 0
 
     def pick(a, b, c):
-        return jnp.where(inside, a, jnp.where(sides, b, c))
-
-    row = pick(n // 3, m, 7)
-    return (row, pick(2 * (n % 3) + 1, 0, 2 * k)), (row, pick(2 * (n % 3) + 2, 7, 2 * k + 1))
-
-
-def near_field(npk, acc, cols_a, cols_b, events):
-    set_columns(npk, cols_a, *near_order(jnp.int32(0))[0])
-
+        return jnp.where(border, jnp.where(sides, b, c), a)
+
+    row = pick(middle // 3, side, 7)
+    return (row, pick(2 * (middle % 3) + 1, 0, 2 * last)), (row, pick(2 * (middle % 3) + 2, 7, 2 * last + 1))
+
+
+def near_step(npk, acc, cols_a, cols_b, n, beside=None):
+    n = jnp.int32(n)
+    first, second = near_order(n)
+    set_columns(npk, cols_b, *second)
+    near_box(npk, acc, cols_a, *first)
+    set_columns(npk, cols_a, *near_order(jnp.minimum(n + 1, 31))[0])
+    if beside is not None:
+        beside()
+    near_box(npk, acc, cols_b, *second)
+
+
+def near_loop(npk, acc, cols_a, cols_b, low, high, events):
     def body(n, _):
         for step, event in events:
             pl.when(n == step)(event)
-        first, second = near_order(n)
-        set_columns(npk, cols_b, *second)
-        near_box(npk, acc, cols_a, *first)
-        set_columns(npk, cols_a, *near_order(jnp.minimum(n + 1, 31))[0])
-        near_box(npk, acc, cols_b, *second)
+        near_step(npk, acc, cols_a, cols_b, n)
         return 0
 
-    lax.fori_loop(0, 32, body, 0)
+    lax.fori_loop(low, high, body, 0)
 
 
 def own_coefficients(vec, basis, i):
@@ -163,7 +168,7 @@
 
 
 def four(ref, m, n):
-    return ref[2 * m : 2 * m + 2, 2 * n : 2 * n + 2].reshape(4 * ref.shape[2], ref.shape[3])
+    return ref[pl.ds(2 * m, 2), pl.ds(2 * n, 2)].reshape(4 * ref.shape[2], ref.shape[3])
 
 
 def far_single(window, couple, bit_x, bit_y):
@@ -199,7 +204,7 @@
 
 
 def kernel(*refs):
-    given, out, (npk, f, ga, gb, g2, acc, cols_a, cols_b, back_s, back_r, back_c, result, send, recv, sends, recvs, send3, recv3, load, store) = refs[:13], refs[13], refs[27:]
+    given, out, (npk, f, ga, gb, g2, acc, cols_a, cols_b, back_s, back_r, back_c, result, lv0, lv0m, part1, send, recv, sends, recvs, send3, recv3, load, store) = refs[:13], refs[13], refs[27:]
     held = refs[14:27]
     off, vec, basis, cp0, cp1, cp2, cp3, cp4, cpt, tr1, tr2, tr3, tr4 = held
     gx, gy = lax.axis_index("gx"), lax.axis_index("gy")
@@ -273,19 +278,24 @@
 
     lax.fori_loop(0, 8, pack, 0)
 
-    c0 = [own_coefficients(vec, basis, i) for i in range(8)]
-    for m, at in enumerate((4, 3, 9, 8)):
-        f[at, :, 128:384] = jnp.concatenate([c0[2 * m], c0[2 * m + 1]], axis=0).astype(BF)
-    c1 = [row_up(c0[2 * m], c0[2 * m + 1], tr1, m, 4) for m in range(4)]
-    blank = jnp.zeros((8, 64), F32)
-    c2 = [jnp.concatenate([row_up(c1[2 * m], c1[2 * m + 1], tr2, m, 2), blank], axis=1) for m in range(2)]
-    for at, upper, lower in ((5, c1[0], c1[1]), (6, c2[0], c2[1]), (7, c1[2], c1[3])):
-        block = jnp.concatenate([upper, lower], axis=0).astype(BF)
-        f[at, :, 128:256] = block
-        f[at, :, 256:384] = block
-    c3 = row_up(c2[0], c2[1], tr3, 0, 1)
-    mine = jnp.concatenate([c3] * 4, axis=1)
-    ga[gy % 4] = jnp.where(lane((8, 128)) // 32 == gy % 4, mine, 0.0)
+    def coefficients():
+        c0 = [own_coefficients(vec, basis, i) for i in range(8)]
+        for m, at in enumerate((4, 3, 9, 8)):
+            f[at, :, 128:384] = jnp.concatenate([c0[2 * m], c0[2 * m + 1]], axis=0).astype(BF)
+        c1 = [row_up(c0[2 * m], c0[2 * m + 1], tr1, m, 4) for m in range(4)]
+        blank = jnp.zeros((8, 64), F32)
+        c2 = [jnp.concatenate([row_up(c1[2 * m], c1[2 * m + 1], tr2, m, 2), blank], axis=1) for m in range(2)]
+        for at, upper, lower in ((5, c1[0], c1[1]), (6, c2[0], c2[1]), (7, c1[2], c1[3])):
+            block = jnp.concatenate([upper, lower], axis=0).astype(BF)
+            f[at, :, 128:256] = block
+            f[at, :, 256:384] = block
+        c3 = row_up(c2[0], c2[1], tr3, 0, 1)
+        mine = jnp.concatenate([c3] * 4, axis=1)
+        ga[gy % 4] = jnp.where(lane((8, 128)) // 32 == gy % 4, mine, 0.0)
+
+    acc[...] = jnp.zeros(acc.shape, F32)
+    set_columns(npk, cols_a, *near_order(jnp.int32(0))[0])
+    near_step(npk, acc, cols_a, cols_b, 0, coefficients)
 
     pl.semaphore_wait(barrier, peers)
 
@@ -362,7 +372,6 @@
             for c in copies:
                 c.start()
 
-    acc[...] = jnp.zeros(acc.shape, F32)
 
     def after_a():
         end_stage(0)
@@ -389,77 +398,110 @@
                 for c in copies:
                     c.wait_recv()
 
-    near_field(npk, acc, cols_a, cols_b, [(5, after_a), (10, after_b), (15, after_c), (21, arrived)])
-    for a, b in BACK:
-        ok, back = back_copies(a, b)
-
-        @pl.when(ok)
-        def _():
-            back.start()
-
+    def give_back():
+        for a, b in BACK:
+            ok, back = back_copies(a, b)
+
+            @pl.when(ok)
+            def _():
+                back.start()
+
+    near_loop(npk, acc, cols_a, cols_b, 1, 27, [(4, after_a), (8, after_b), (10, arrived), (12, after_c), (21, give_back)])
     for n in range(13):
         if n not in first:
             loads[n].wait()
     end_stage(3)
 
-    whole3 = g2[...].astype(F32)
-    rows3 = [jnp.concatenate([whole3[i, 0:8], whole3[i, 8:16]], axis=1) for i in range(NX)]
-    rows4 = [row_up(rows3[2 * m], rows3[2 * m + 1], tr4, m, NY // 2) for m in range(NX // 2)]
-
-    def select(rows, r):
-        got = rows[0]
-        for t in range(1, len(rows)):
-            got = jnp.where(r == t, rows[t], got)
-        return got
-
-    def read3(r):
-        block = g2[r].astype(F32)
-        return jnp.concatenate([block[0:8], block[8:16]], axis=1)
-
-    far3 = far_single(single_window(read3, NX, 32 * NY, gx, gy), cp3[0, 0], gx % 2, gy % 2)
-    window4 = single_window(lambda r: select(rows4, r), NX // 2, 16 * NY, anc_x, anc_y)
-    down4 = far_single(window4, cp4[...], anc_x % 2, anc_y % 2)
-    base_x, base_y = 2 * (anc_x // 2), 2 * (anc_y // 2)
-    box_y = lane((8, 16 * NY)) // 32
-    near_y = (box_y >= base_y - 2) & (box_y <= base_y + 3)
-    masked = []
-    for m in range(NX // 2):
-        near_x = (m >= base_x - 2) & (m <= base_x + 3)
-        masked.append(jnp.where(near_y & near_x, 0.0, rows4[m]))
-    top = dot_t(jnp.concatenate(masked, axis=1).astype(BF), cpt[0, 0])
-    slot = 2 * (gx % 2) + gy % 2
-    own4 = dot_t(down4.astype(BF), tr4[anc_x, anc_y, slot])
-    down3 = far3 + top + own4
-
-    tiles = [f[0].astype(F32), f[6].astype(F32), f[12].astype(F32)]
-    window = []
-    for t in tiles:
-        wide = jnp.concatenate([t[:, 0:64], t[:, 128:192], t[:, 384:448]], axis=1)
-        window += [wide[0:8], wide[8:16]]
-    down2 = far_parent(window, four(cp2, 0, 0)) + spread(down3, tr3[0, 0])
-
-    rows = []
-    for t in (1, 5, 7, 11):
-        block = f[t].astype(F32)
-        block = jnp.concatenate([block[:, 0:256], block[:, 384:512]], axis=1)
-        rows += [block[0:8], block[8:16]]
-    moved = [shifted(row) for row in rows]
-    down1 = {}
-    for m in range(2):
-        for n in range(2):
-            window = []
-            for a in range(6):
+    def coarse():
+        whole3 = g2[...].astype(F32)
+        rows3 = [jnp.concatenate([whole3[i, 0:8], whole3[i, 8:16]], axis=1) for i in range(NX)]
+        rows4 = [row_up(rows3[2 * m], rows3[2 * m + 1], tr4, m, NY // 2) for m in range(NX // 2)]
+
+        def select(rows, r):
+            got = rows[0]
+            for t in range(1, len(rows)):
+                got = jnp.where(r == t, rows[t], got)
+            return got
+
+        def read3(r):
+            block = g2[r].astype(F32)
+            return jnp.concatenate([block[0:8], block[8:16]], axis=1)
+
+        far3 = far_single(single_window(read3, NX, 32 * NY, gx, gy), cp3[0, 0], gx % 2, gy % 2)
+        window4 = single_window(lambda r: select(rows4, r), NX // 2, 16 * NY, anc_x, anc_y)
+        down4 = far_single(window4, cp4[...], anc_x % 2, anc_y % 2)
+        base_x, base_y = 2 * (anc_x // 2), 2 * (anc_y // 2)
+        box_y = lane((8, 16 * NY)) // 32
+        near_y = (box_y >= base_y - 2) & (box_y <= base_y + 3)
+        masked = []
+        for m in range(NX // 2):
+            near_x = (m >= base_x - 2) & (m <= base_x + 3)
+            masked.append(jnp.where(near_y & near_x, 0.0, rows4[m]))
+        top = dot_t(jnp.concatenate(masked, axis=1).astype(BF), cpt[0, 0])
+        slot = 2 * (gx % 2) + gy % 2
+        own4 = dot_t(down4.astype(BF), tr4[anc_x, anc_y, slot])
+        down3 = far3 + top + own4
+
+        tiles = [f[0].astype(F32), f[6].astype(F32), f[12].astype(F32)]
+        window = []
+        for t in tiles:
+            wide = jnp.concatenate([t[:, 0:64], t[:, 128:192], t[:, 384:448]], axis=1)
+            window += [wide[0:8], wide[8:16]]
+        down2 = far_parent(window, four(cp2, 0, 0)) + spread(down3, tr3[0, 0])
+
+        rows = []
+        for t in (1, 5, 7, 11):
+            block = f[t].astype(F32)
+            block = jnp.concatenate([block[:, 0:256], block[:, 384:512]], axis=1)
+            rows += [block[0:8], block[8:16]]
+        moved = [shifted(row) for row in rows]
+        down1 = {}
+        for m in range(2):
+            for n in range(2):
+                window = []
+                for a in range(6):
+                    at = 64 + 64 * n
+                    window.append(rows[2 * m + a][:, at : at + 256] if at % 128 == 0 else moved[2 * m + a][:, at - 64 : at + 192])
+                far = far_parent(window, four(cp1, m, n))
+                down1[m, n] = far + spread(slot_part(down2, 2 * m + n), tr2[m, n])
+
+        for m in range(4):
+            for n in range(4):
+                s = 2 * (m % 2) + n % 2
+                given1 = down1[m // 2, n // 2]
+                part1[m, n] = pltpu.roll(given1, 128 - 32 * s, 1) if s else given1
+
+        for k, t in enumerate((2, 4, 3, 9, 8, 10)):
+            block = f[t].astype(F32)
+            for h in range(2):
+                lv0[2 * k + h] = block[8 * h : 8 * h + 8]
+                lv0m[2 * k + h] = shifted(block[8 * h : 8 * h + 8])
+
+    near_step(npk, acc, cols_a, cols_b, 27, coarse)
+    group = lane((8, 128)) // 32
+    scale = 0.0625 * ROOT3
+
+    def finest(m, _):
+        def row():
+            for n in range(4):
                 at = 64 + 64 * n
-                window.append(rows[2 * m + a][:, at : at + 256] if at % 128 == 0 else moved[2 * m + a][:, at - 64 : at + 192])
-            far = far_parent(window, four(cp1, m, n))
-            down1[m, n] = far + spread(slot_part(down2, 2 * m + n), tr2[m, n])
-
-    rows = []
-    for t in (2, 4, 3, 9, 8, 10):
-        block = f[t].astype(F32)
-        rows += [block[0:8], block[8:16]]
-    moved = [shifted(row) for row in rows]
-    group = lane((8, 128)) // 32
+                window = []
+                for a in range(6):
+                    if at % 128 == 0:
+                        window.append(lv0[2 * m + a, :, at : at + 256])
+                    else:
+                        window.append(lv0m[2 * m + a, :, at - 64 : at + 192])
+                far = far_parent(window, four(cp0, m, n))
+                down0 = far + spread(part1[m, n][:, :32], tr1[m, n])
+                parts = jnp.concatenate([jnp.where(group == t, down0, 0.0) for t in range(4)], axis=0).astype(BF)
+                given0 = dot_n(parts, four(basis, m, n)) * (1.0 / scale)
+                for t in range(4):
+                    acc[2 * m + t // 2, 1 + 2 * n + t % 2] += given0[8 * t : 8 * t + 8]
+
+        near_step(npk, acc, cols_a, cols_b, 28 + m, row)
+        return 0
+
+    lax.fori_loop(0, 4, finest, 0)
     for a, b in BACK:
         back = back_copies(a, b)[1]
 
@@ -468,33 +510,24 @@
             back.wait_recv()
 
     stores = []
-    for m in range(4):
-        for n in range(4):
-            window = []
-            for a in range(6):
-                at = 64 + 64 * n
-                window.append(rows[2 * m + a][:, at : at + 256] if at % 128 == 0 else moved[2 * m + a][:, at - 64 : at + 192])
-            far = far_parent(window, four(cp0, m, n))
-            s = 2 * (m % 2) + n % 2
-            down0 = far + spread(slot_part(down1[m // 2, n // 2], s), tr1[m, n])
-            parts = jnp.concatenate([jnp.where(group == t, down0, 0.0) for t in range(4)], axis=0).astype(BF)
-            given = dot_n(parts, four(basis, m, n))
-            for t in range(4):
-                i, j = 2 * m + t // 2, 2 * n + t % 2
-                near = acc[i, j + 1]
-                if j == 0:
-                    near = near + back_s[0, i]
-                if j == 7:
-                    near = near + back_s[1, i]
-                if i == 0:
-                    near = near + back_r[j]
-                if (i, j) == (0, 0):
-                    near = near + back_c[0]
-                if (i, j) == (0, 7):
-                    near = near + back_c[1]
-                result[i, j] = near * (0.0625 * ROOT3) + given[8 * t : 8 * t + 8]
-        stores.append(pltpu.make_async_copy(result.at[pl.ds(2 * m, 2)], out.at[pl.ds(2 * m, 2)], store.at[m]))
-        stores[m].start()
+    for i in range(8):
+        for j in range(8):
+            near = acc[i, j + 1]
+            if j == 0:
+                near = near + back_s[0, i]
+            if j == 7:
+                near = near + back_s[1, i]
+            if i == 0:
+                near = near + back_r[j]
+            if (i, j) == (0, 0):
+                near = near + back_c[0]
+            if (i, j) == (0, 7):
+                near = near + back_c[1]
+            result[i, j] = near * scale
+        if i % 2:
+            m = i // 2
+            stores.append(pltpu.make_async_copy(result.at[pl.ds(2 * m, 2)], out.at[pl.ds(2 * m, 2)], store.at[m]))
+            stores[m].start()
 
     for a, b in SIDES:
         ok, copies = side_copies(a, b)
@@ -543,6 +576,9 @@
             pltpu.VMEM((8, 8, 256), F32),
             pltpu.VMEM((2, 8, 256), F32),
             pltpu.VMEM((8, 8, 8, 256), F32),
+            pltpu.VMEM((12, 8, 512), F32),
+            pltpu.VMEM((12, 8, 512), F32),
+            pltpu.VMEM((4, 4, 8, 128), F32),
             sem((8, 2)),
             sem((8, 2)),
             sem((4, 4)),

time: 48.5 us -> 47.4 us (0.977)
  Pallas kernels: 46.5 us -> 45 us
    pallas_call x1, Pallas kernels: 46.5 us -> 45 us  [on_device(): pl.pallas_call(kernel, out_shape=jax.ShapeDtypeStruct((8, 8, 8, 256), F32...]
where the time goes in v5:
time: 47.4 us; the launch traced here: 46.9 us
  Pallas kernels  45 us (95%)
  local copies, waits for them, and re-layouts  1.87 us (4%)
    pallas_call x1, Pallas kernels, on_device(): pl.pallas_call(kernel, out_shape=jax.ShapeDtypeStruct((8, 8, 8, 256), F32...  45 us
    unnamed x1, local copies, waits for them, and re-layouts  1.87 us

profile of v5, /device:TPU:1, one launch (start us, length us, event | category | flops | bytes accessed | tf_op | source)
XLA Modules:
  0.0 46.9 jit_solution(2356963893977488959)
XLA Ops:
  0.0 45.0 %product.1 = f32[8,8,8,256]{3,2,1,0:T(8,128)} custom-call(bf16[8,8,2,256]{3,2,1,0:T(2,128)(2,1)} %refs_0_.1, bf16[8,8,8,256]{3,2,1,0:T(8,128)(2,1)} %refs_1_.1, bf16[8,8,32,256]{3,2,1,0:T(8,128)(2,1)} %refs_2_.1, bf16[8,8,32,864]{3,2,1,0:T(8,128)(2,1)} %refs_3_.1, bf16[4,4,32,864]{3,2,1,0:T(8,128)(2,1)} %refs_4_.1, bf16[2,2,32,864]{3,2,1,0:T(8,128)(2,1)} %refs_5_.1, ...), custom_call_target="tpu_custom_call" | custom-call | tf_op jit(solution)/shard_map/product/pallas_call | solution.py:560
  45.0 1.9 %copy.15 = f32[8,8,8,256]{3,2,1,0:T(8,128)} copy(f32[8,8,8,256]{3,2,1,0:T(8,128)} %product.1) | data formatting | bytes 1048576

commit v6 on v5

--- a/solution.py
+++ b/solution.py
@@ -84,8 +84,8 @@
 
 
 def near_order(n):
-    middle, side, last = n - 11 * (n // 21), n - 10, n - 17
-    border, sides = (n // 10 >= 1) & (n // 21 == 0), n // 17 == 0
+    middle, side, last = n - 11 * (n // 26), n - 15, n - 22
+    border, sides = (n // 15 >= 1) & (n // 26 == 0), n // 22 == 0
 
     def pick(a, b, c):
         return jnp.where(border, jnp.where(sides, b, c), a)
@@ -204,7 +204,7 @@
 
 
 def kernel(*refs):
-    given, out, (npk, f, ga, gb, g2, acc, cols_a, cols_b, back_s, back_r, back_c, result, lv0, lv0m, part1, send, recv, sends, recvs, send3, recv3, load, store) = refs[:13], refs[13], refs[27:]
+    given, out, (npk, f, ga, g2, acc, cols_a, cols_b, back_s, back_r, back_c, result, lv0, lv0m, part1, send, recv, sends, recvs, send3, recv3, load, store) = refs[:13], refs[13], refs[27:]
     held = refs[14:27]
     off, vec, basis, cp0, cp1, cp2, cp3, cp4, cpt, tr1, tr2, tr3, tr4 = held
     gx, gy = lax.axis_index("gx"), lax.axis_index("gy")
@@ -238,27 +238,15 @@
 
     def partner(stage, k):
         if stage == 0:
-            return gx, 4 * (gy // 4) + (gy + k) % 4
-        if stage == 1:
-            return gx, (gy + 4 * k) % NY
-        if stage == 2:
-            return 4 * (gx // 4) + (gx + k) % 4, gy
-        return (gx + 4 * k) % NX, gy
-
-    def greeted(a, b):
+            return gx, (gy + k) % NY
+        return (gx + k) % NX, gy
+
+    for stage in range(2):
+        for k in range(1, 16):
+            pl.semaphore_signal(barrier, inc=1, device_id=partner(stage, k), device_id_type=MESH)
+    peers = jnp.int32(30)
+    for a, b in [(-1, -1), (-1, 1), (1, -1), (1, 1)]:
         ok, x, y = there(a, b)
-        if not a:
-            ok = ok & (gy % 4 == (3 if b > 0 else 0))
-        if not b:
-            ok = ok & (gx % 4 == (3 if a > 0 else 0))
-        return ok, x, y
-
-    for stage in range(4):
-        for k in range(1, 4):
-            pl.semaphore_signal(barrier, inc=1, device_id=partner(stage, k), device_id_type=MESH)
-    peers = jnp.int32(12)
-    for a, b in SIDES:
-        ok, x, y = greeted(a, b)
         peers = peers + ok.astype(jnp.int32)
 
         @pl.when(ok)
@@ -291,29 +279,20 @@
             f[at, :, 256:384] = block
         c3 = row_up(c2[0], c2[1], tr3, 0, 1)
         mine = jnp.concatenate([c3] * 4, axis=1)
-        ga[gy % 4] = jnp.where(lane((8, 128)) // 32 == gy % 4, mine, 0.0)
+        ga[gy] = jnp.where(lane((8, 128)) // 32 == gy % 4, mine, 0.0)
 
     acc[...] = jnp.zeros(acc.shape, F32)
     set_columns(npk, cols_a, *near_order(jnp.int32(0))[0])
     near_step(npk, acc, cols_a, cols_b, 0, coefficients)
 
-    pl.semaphore_wait(barrier, peers)
-
     def stage_copies(stage):
-        if stage == 0:
-            ref = ga.at[gy % 4]
-        elif stage == 1:
-            ref = gb.at[gy // 4]
-        elif stage == 2:
-            ref = g2.at[gx]
-        else:
-            ref = g2.at[pl.ds(4 * (gx // 4), 4)]
+        ref = g2.at[gx] if stage else ga.at[gy]
         return [
             pltpu.make_async_remote_copy(
-                src_ref=ref, dst_ref=ref, send_sem=sends.at[stage, k], recv_sem=recvs.at[stage, 4 - k],
+                src_ref=ref, dst_ref=ref, send_sem=sends.at[stage, k], recv_sem=recvs.at[stage, 16 - k],
                 device_id=partner(stage, k), device_id_type=MESH,
             )
-            for k in range(1, 4)
+            for k in range(1, 16)
         ]
 
     def start_stage(stage):
@@ -323,8 +302,6 @@
     def end_stage(stage):
         for c in stage_copies(stage):
             c.wait_recv()
-
-    start_stage(0)
 
     def side_copies(a, b):
         ok, x, y = there(a, b)
@@ -364,30 +341,23 @@
             device_id=(x, y), device_id_type=MESH,
         )
 
-    for a, b in SIDES:
-        ok, copies = side_copies(a, b)
-
-        @pl.when(ok)
-        def _():
-            for c in copies:
-                c.start()
-
+    def send_all():
+        pl.semaphore_wait(barrier, peers)
+        start_stage(0)
+        for a, b in SIDES:
+            ok, copies = side_copies(a, b)
+
+            @pl.when(ok)
+            def _():
+                for c in copies:
+                    c.start()
 
     def after_a():
         end_stage(0)
-        gb[gy // 4] = ga[0] + ga[1] + ga[2] + ga[3]
+        groups = [ga[4 * t] + ga[4 * t + 1] + ga[4 * t + 2] + ga[4 * t + 3] for t in range(4)]
+        upper, lower = jnp.concatenate(groups[0:2], axis=1), jnp.concatenate(groups[2:4], axis=1)
+        g2[gx] = jnp.concatenate([upper, lower], axis=0).astype(BF)
         start_stage(1)
-
-    def after_b():
-        end_stage(1)
-        upper = jnp.concatenate([gb[0], gb[1]], axis=1)
-        lower = jnp.concatenate([gb[2], gb[3]], axis=1)
-        g2[gx] = jnp.concatenate([upper, lower], axis=0).astype(BF)
-        start_stage(2)
-
-    def after_c():
-        end_stage(2)
-        start_stage(3)
 
     def arrived():
         for a, b in SIDES:
@@ -406,11 +376,11 @@
             def _():
                 back.start()
 
-    near_loop(npk, acc, cols_a, cols_b, 1, 27, [(4, after_a), (8, after_b), (10, arrived), (12, after_c), (21, give_back)])
+    near_loop(npk, acc, cols_a, cols_b, 1, 27, [(3, send_all), (15, after_a), (15, arrived), (26, give_back)])
     for n in range(13):
         if n not in first:
             loads[n].wait()
-    end_stage(3)
+    end_stage(1)
 
     def coarse():
         whole3 = g2[...].astype(F32)
@@ -544,7 +514,7 @@
         def _():
             back.wait_send()
 
-    for stage in range(4):
+    for stage in range(2):
         for c in stage_copies(stage):
             c.wait_send()
     for c in stores:
@@ -566,8 +536,7 @@
         + [
             pltpu.VMEM((9, 10, 16, 256), BF),
             pltpu.VMEM((13, 16, 512), BF),
-            pltpu.VMEM((4, 8, 128), F32),
-            pltpu.VMEM((4, 8, 128), F32),
+            pltpu.VMEM((NY, 8, 128), F32),
             pltpu.VMEM((NX, 16, 256), BF),
             pltpu.VMEM((9, 10, 8, 256), F32),
             pltpu.VMEM((4, 256, 128), BF),
@@ -581,8 +550,8 @@
             pltpu.VMEM((4, 4, 8, 128), F32),
             sem((8, 2)),
             sem((8, 2)),
-            sem((4, 4)),
-            sem((4, 4)),
+            sem((2, 16)),
+            sem((2, 16)),
             sem((5,)),
             sem((5,)),
             sem((13,)),

time: 47.4 us -> 43.3 us (0.914)
  Pallas kernels: 45 us -> 41.3 us
    pallas_call x1, Pallas kernels: 45 us -> 41.3 us  [on_device(): pl.pallas_call(kernel, out_shape=jax.ShapeDtypeStruct((8, 8, 8, 256), F32...]
where the time goes in v6:
time: 43.3 us; the launch traced here: 43.2 us
  Pallas kernels  41.3 us (95%)
  local copies, waits for them, and re-layouts  1.87 us (4%)
    pallas_call x1, Pallas kernels, on_device(): pl.pallas_call(kernel, out_shape=jax.ShapeDtypeStruct((8, 8, 8, 256), F32...  41.3 us
    unnamed x1, local copies, waits for them, and re-layouts  1.87 us

profile of v6, /device:TPU:1, one launch (start us, length us, event | category | flops | bytes accessed | tf_op | source)
XLA Modules:
  0.0 43.2 jit_solution(9723596553284370231)
XLA Ops:
  0.0 41.3 %product.1 = f32[8,8,8,256]{3,2,1,0:T(8,128)} custom-call(bf16[8,8,2,256]{3,2,1,0:T(2,128)(2,1)} %refs_0_.1, bf16[8,8,8,256]{3,2,1,0:T(8,128)(2,1)} %refs_1_.1, bf16[8,8,32,256]{3,2,1,0:T(8,128)(2,1)} %refs_2_.1, bf16[8,8,32,864]{3,2,1,0:T(8,128)(2,1)} %refs_3_.1, bf16[4,4,32,864]{3,2,1,0:T(8,128)(2,1)} %refs_4_.1, bf16[2,2,32,864]{3,2,1,0:T(8,128)(2,1)} %refs_5_.1, ...), custom_call_target="tpu_custom_call" | custom-call | tf_op jit(solution)/shard_map/product/pallas_call | solution.py:530
  41.3 1.9 %copy.15 = f32[8,8,8,256]{3,2,1,0:T(8,128)} copy(f32[8,8,8,256]{3,2,1,0:T(8,128)} %product.1) | data formatting | bytes 1048576

commit v7 on v6

--- a/solution.py
+++ b/solution.py
@@ -84,8 +84,8 @@
 
 
 def near_order(n):
-    middle, side, last = n - 11 * (n // 26), n - 15, n - 22
-    border, sides = (n // 15 >= 1) & (n // 26 == 0), n // 22 == 0
+    middle, side, last = n - 11 * (n // 27), n - 16, n - 23
+    border, sides = (n // 16 >= 1) & (n // 27 == 0), n // 23 == 0
 
     def pick(a, b, c):
         return jnp.where(border, jnp.where(sides, b, c), a)
@@ -221,14 +221,16 @@
     for n in range(13):
         src = given[n].at[anc_x, anc_y] if n == 7 else given[n]
         loads.append(pltpu.make_async_copy(src, held[n], load.at[n]))
-    first = (0, 1, 2, 9, 10, 11)
+    first, second = (0, 1), (2, 9, 10, 11)
     for n in first:
         loads[n].start()
-    for n in range(13):
-        if n not in first:
-            loads[n].start()
-
-    npk[...] = jnp.zeros(npk.shape, BF)
+    for n in second:
+        loads[n].start()
+
+    npk[8] = jnp.zeros((10, 16, 256), BF)
+    for i in range(8):
+        npk[i, 0] = jnp.zeros((16, 256), BF)
+        npk[i, 9] = jnp.zeros((16, 256), BF)
     f[...] = jnp.zeros(f.shape, BF)
     back_s[...] = jnp.zeros(back_s.shape, F32)
     back_r[...] = jnp.zeros(back_r.shape, F32)
@@ -253,6 +255,9 @@
         def _():
             pl.semaphore_signal(barrier, inc=1, device_id=(x, y), device_id_type=MESH)
 
+    for n in range(13):
+        if n not in first + second:
+            loads[n].start()
     for n in first:
         loads[n].wait()
 
@@ -283,7 +288,10 @@
 
     acc[...] = jnp.zeros(acc.shape, F32)
     set_columns(npk, cols_a, *near_order(jnp.int32(0))[0])
-    near_step(npk, acc, cols_a, cols_b, 0, coefficients)
+    near_step(npk, acc, cols_a, cols_b, 0)
+    for n in second:
+        loads[n].wait()
+    near_step(npk, acc, cols_a, cols_b, 1, coefficients)
 
     def stage_copies(stage):
         ref = g2.at[gx] if stage else ga.at[gy]
@@ -376,9 +384,10 @@
             def _():
                 back.start()
 
-    near_loop(npk, acc, cols_a, cols_b, 1, 27, [(3, send_all), (15, after_a), (15, arrived), (26, give_back)])
+    near_loop(npk, acc, cols_a, cols_b, 2, 27, [(5, send_all), (16, after_a), (16, arrived)])
+    give_back()
     for n in range(13):
-        if n not in first:
+        if n not in first + second:
             loads[n].wait()
     end_stage(1)
 

time: 43.3 us -> 41.3 us (0.954)
  Pallas kernels: 41.3 us -> 39.3 us
    pallas_call x1, Pallas kernels: 41.3 us -> 39.3 us  [on_device(): pl.pallas_call(kernel, out_shape=jax.ShapeDtypeStruct((8, 8, 8, 256), F32...]
where the time goes in v7:
time: 41.3 us; the launch traced here: 41.2 us
  Pallas kernels  39.3 us (95%)
  local copies, waits for them, and re-layouts  1.87 us (5%)
    pallas_call x1, Pallas kernels, on_device(): pl.pallas_call(kernel, out_shape=jax.ShapeDtypeStruct((8, 8, 8, 256), F32...  39.3 us
    unnamed x1, local copies, waits for them, and re-layouts  1.87 us

profile of v7, /device:TPU:1, one launch (start us, length us, event | category | flops | bytes accessed | tf_op | source)
XLA Modules:
  0.0 41.2 jit_solution(15714127657323687333)
XLA Ops:
  0.0 39.3 %product.1 = f32[8,8,8,256]{3,2,1,0:T(8,128)} custom-call(bf16[8,8,2,256]{3,2,1,0:T(2,128)(2,1)} %refs_0_.1, bf16[8,8,8,256]{3,2,1,0:T(8,128)(2,1)} %refs_1_.1, bf16[8,8,32,256]{3,2,1,0:T(8,128)(2,1)} %refs_2_.1, bf16[8,8,32,864]{3,2,1,0:T(8,128)(2,1)} %refs_3_.1, bf16[4,4,32,864]{3,2,1,0:T(8,128)(2,1)} %refs_4_.1, bf16[2,2,32,864]{3,2,1,0:T(8,128)(2,1)} %refs_5_.1, ...), custom_call_target="tpu_custom_call" | custom-call | tf_op jit(solution)/shard_map/product/pallas_call | solution.py:539
  39.3 1.9 %copy.15 = f32[8,8,8,256]{3,2,1,0:T(8,128)} copy(f32[8,8,8,256]{3,2,1,0:T(8,128)} %product.1) | data formatting | bytes 1048576

commit v8 on v7

--- a/solution.py
+++ b/solution.py
@@ -165,6 +165,20 @@
 def far_parent(window, couple4):
     stacks = [class_stack(window, px, py) for px in range(2) for py in range(2)]
     return diagonal(dot_t(jnp.concatenate(stacks, axis=0).astype(BF), couple4))
+
+
+def far_two(windows, couples):
+    both = [jnp.concatenate([a, b], axis=0).astype(BF) for a, b in zip(*windows)]
+    stacks = jnp.concatenate([class_stack(both, px, py) for px in range(2) for py in range(2)], axis=0)
+    group = lane((8, 128)) // 32
+    fars = []
+    for h in range(2):
+        o = dot_t(stacks, couples[h])
+        far = o[8 * h : 8 * h + 8]
+        for s in range(1, 4):
+            far = jnp.where(group == s, o[16 * s + 8 * h : 16 * s + 8 * h + 8], far)
+        fars.append(far)
+    return fars
 
 
 def four(ref, m, n):
@@ -462,15 +476,18 @@
 
     def finest(m, _):
         def row():
+            fars = []
+            for half in range(2):
+                windows = []
+                for n in (2 * half, 2 * half + 1):
+                    at = 64 + 64 * n
+                    if at % 128 == 0:
+                        windows.append([lv0[2 * m + a, :, at : at + 256] for a in range(6)])
+                    else:
+                        windows.append([lv0m[2 * m + a, :, at - 64 : at + 192] for a in range(6)])
+                fars += far_two(windows, [four(cp0, m, 2 * half), four(cp0, m, 2 * half + 1)])
             for n in range(4):
-                at = 64 + 64 * n
-                window = []
-                for a in range(6):
-                    if at % 128 == 0:
-                        window.append(lv0[2 * m + a, :, at : at + 256])
-                    else:
-                        window.append(lv0m[2 * m + a, :, at - 64 : at + 192])
-                far = far_parent(window, four(cp0, m, n))
+                far = fars[n]
                 down0 = far + spread(part1[m, n][:, :32], tr1[m, n])
                 parts = jnp.concatenate([jnp.where(group == t, down0, 0.0) for t in range(4)], axis=0).astype(BF)
                 given0 = dot_n(parts, four(basis, m, n)) * (1.0 / scale)

time: 41.3 us -> 40.6 us (0.983)
  Pallas kernels: 39.3 us -> 38.6 us
    pallas_call x1, Pallas kernels: 39.3 us -> 38.6 us  [on_device(): pl.pallas_call(kernel, out_shape=jax.ShapeDtypeStruct((8, 8, 8, 256), F32...]
where the time goes in v8:
time: 40.6 us; the launch traced here: 40.5 us
  Pallas kernels  38.6 us (95%)
  local copies, waits for them, and re-layouts  1.87 us (5%)
    pallas_call x1, Pallas kernels, on_device(): pl.pallas_call(kernel, out_shape=jax.ShapeDtypeStruct((8, 8, 8, 256), F32...  38.6 us
    unnamed x1, local copies, waits for them, and re-layouts  1.87 us

profile of v8, /device:TPU:1, one launch (start us, length us, event | category | flops | bytes accessed | tf_op | source)
XLA Modules:
  0.0 40.5 jit_solution(5864066079572976815)
XLA Ops:
  0.0 38.6 %product.1 = f32[8,8,8,256]{3,2,1,0:T(8,128)} custom-call(bf16[8,8,2,256]{3,2,1,0:T(2,128)(2,1)} %refs_0_.1, bf16[8,8,8,256]{3,2,1,0:T(8,128)(2,1)} %refs_1_.1, bf16[8,8,32,256]{3,2,1,0:T(8,128)(2,1)} %refs_2_.1, bf16[8,8,32,864]{3,2,1,0:T(8,128)(2,1)} %refs_3_.1, bf16[4,4,32,864]{3,2,1,0:T(8,128)(2,1)} %refs_4_.1, bf16[2,2,32,864]{3,2,1,0:T(8,128)(2,1)} %refs_5_.1, ...), custom_call_target="tpu_custom_call" | custom-call | tf_op jit(solution)/shard_map/product/pallas_call | solution.py:556
  38.6 1.9 %copy.15 = f32[8,8,8,256]{3,2,1,0:T(8,128)} copy(f32[8,8,8,256]{3,2,1,0:T(8,128)} %product.1) | data formatting | bytes 1048576

commit v9 on v8

--- a/solution.py
+++ b/solution.py
@@ -398,7 +398,7 @@
             def _():
                 back.start()
 
-    near_loop(npk, acc, cols_a, cols_b, 2, 27, [(5, send_all), (16, after_a), (16, arrived)])
+    near_loop(npk, acc, cols_a, cols_b, 2, 27, [(6, send_all), (16, arrived), (16, after_a)])
     give_back()
     for n in range(13):
         if n not in first + second:
@@ -450,12 +450,15 @@
         moved = [shifted(row) for row in rows]
         down1 = {}
         for m in range(2):
+            windows = []
             for n in range(2):
-                window = []
-                for a in range(6):
-                    at = 64 + 64 * n
-                    window.append(rows[2 * m + a][:, at : at + 256] if at % 128 == 0 else moved[2 * m + a][:, at - 64 : at + 192])
-                far = far_parent(window, four(cp1, m, n))
+                at = 64 + 64 * n
+                windows.append(
+                    [rows[2 * m + a][:, at : at + 256] if at % 128 == 0 else moved[2 * m + a][:, at - 64 : at + 192] for a in range(6)]
+                )
+            fars = far_two(windows, [four(cp1, m, 0), four(cp1, m, 1)])
+            for n in range(2):
+                far = fars[n]
                 down1[m, n] = far + spread(slot_part(down2, 2 * m + n), tr2[m, n])
 
         for m in range(4):

time: 40.6 us -> 40.3 us (level); the launches traced: 40.5 us -> 39.7 us
  Pallas kernels: 38.6 us -> 37.8 us
    pallas_call x1, Pallas kernels: 38.6 us -> 37.8 us  [on_device(): pl.pallas_call(kernel, out_shape=jax.ShapeDtypeStruct((8, 8, 8, 256), F32...]
where the time goes in v9:
time: 40.3 us; the launch traced here: 39.7 us
  Pallas kernels  37.8 us (94%)
  local copies, waits for them, and re-layouts  1.87 us (5%)
    pallas_call x1, Pallas kernels, on_device(): pl.pallas_call(kernel, out_shape=jax.ShapeDtypeStruct((8, 8, 8, 256), F32...  37.8 us
    unnamed x1, local copies, waits for them, and re-layouts  1.87 us

profile of v9, /device:TPU:1, one launch (start us, length us, event | category | flops | bytes accessed | tf_op | source)
XLA Modules:
  0.0 39.7 jit_solution(1163725769663389444)
XLA Ops:
  0.0 37.8 %product.1 = f32[8,8,8,256]{3,2,1,0:T(8,128)} custom-call(bf16[8,8,2,256]{3,2,1,0:T(2,128)(2,1)} %refs_0_.1, bf16[8,8,8,256]{3,2,1,0:T(8,128)(2,1)} %refs_1_.1, bf16[8,8,32,256]{3,2,1,0:T(8,128)(2,1)} %refs_2_.1, bf16[8,8,32,864]{3,2,1,0:T(8,128)(2,1)} %refs_3_.1, bf16[4,4,32,864]{3,2,1,0:T(8,128)(2,1)} %refs_4_.1, bf16[2,2,32,864]{3,2,1,0:T(8,128)(2,1)} %refs_5_.1, ...), custom_call_target="tpu_custom_call" | custom-call | tf_op jit(solution)/shard_map/product/pallas_call | solution.py:559
  37.8 1.9 %copy.15 = f32[8,8,8,256]{3,2,1,0:T(8,128)} copy(f32[8,8,8,256]{3,2,1,0:T(8,128)} %product.1) | data formatting | bytes 1048576
